TPU v7x, 128 devices: a whole 4x4x4 slice. The times are simulated.
128 devices in a mesh: seq: 16 (over x, y_lo, core), fsdp: 8 (over z, y_hi).
Axes of the slice: x: 4, y: 4 (y_hi: 2, y_lo: 2; y = y_hi * 2 + y_lo), z: 4, core: 2. Of those that a mesh axis runs over, the one named last changes fastest.
Arguments:
- clip_tokens: bfloat16 [16, 256, 3584], P('seq'), may hold values from -6 to 6
- out_cotangent: bfloat16 [16, 256, 3584], P(None, 'seq'), may hold values from -6 to 6
- proj_weight: bfloat16 [2, 3584, 6144], P(None, 'seq', 'fsdp'), may hold values from -0.09375 to 0.09375
- out_weight: bfloat16 [2, 2048, 3584], P(None, 'fsdp', 'seq'), may hold values from -0.125 to 0.125
- norm_gain: float32 [2, 3584], replicated, may hold values from 0.1 to 1.9
- branch_gate: float32 [2, 3584], replicated, may hold values from 0.1 to 1.9
- qk_gain: float32 [2, 2, 128], replicated, may hold values from 0.1 to 1.9
Outputs:
- mixed_out: bfloat16 [16, 256, 3584], P(None, 'seq')
- grad_clip: bfloat16 [16, 256, 3584], P('seq')
- grad_proj: bfloat16 [2, 3584, 6144], P(None, 'seq', 'fsdp')
- grad_outw: bfloat16 [2, 2048, 3584], P(None, 'fsdp', 'seq')
All inputs are finite; a program needn't handle non-finite values.
Results may differ from a plain program's by a relative error of at most 0.035.
Values may be sent and summed in bfloat16 or wider, within the bound.
A program may use at most 128 MiB of HBM per device.

v0:
```python
from functools import partial

import jax
import jax.numpy as jnp
from jax import lax
from jax.sharding import PartitionSpec as P

EPS = 1e-06


def shapes(temporal):
    if temporal:
        return ("lghe,mghe->ghlm", "ghlm,mghe->lghe")
    return ("glhe,gmhe->ghlm", "ghlm,gmhe->glhe")


def unit_norm(values_in, gain):
    return values_in * lax.rsqrt(jnp.mean(values_in * values_in, -1, keepdims=True) + EPS) * gain


def attend(projected, qk_gain, temporal):
    score_form, mix_form = shapes(temporal)
    head_width = projected.shape[-1]
    query_rows = unit_norm(projected[..., 0, :], qk_gain[0]).astype(jnp.bfloat16)
    key_rows = unit_norm(projected[..., 1, :], qk_gain[1]).astype(jnp.bfloat16)
    value_rows = projected[..., 2, :].astype(jnp.bfloat16)
    scores = jnp.einsum(
        score_form, query_rows, key_rows, preferred_element_type=jnp.float32
    ) * head_width ** (-0.5)
    probs = jax.nn.softmax(scores, axis=-1).astype(jnp.bfloat16)
    return jnp.einsum(mix_form, probs, value_rows, preferred_element_type=jnp.float32).astype(
        jnp.bfloat16
    )


def forward_local(inputs, gain, qk_gain, proj_weight, out_weight, temporal):
    head_width = qk_gain.shape[-1]
    local_heads = out_weight.shape[0] // head_width
    widened = inputs.astype(jnp.float32)
    inverse = lax.rsqrt(jnp.mean(widened * widened, -1, keepdims=True) + EPS)
    normed = (widened * inverse * gain).astype(jnp.bfloat16)
    projected = jnp.dot(normed, proj_weight, preferred_element_type=jnp.float32)
    projected = projected.reshape(inputs.shape[0], inputs.shape[1], local_heads, 3, head_width)
    attended = attend(projected, qk_gain, temporal).reshape(
        inputs.shape[0], inputs.shape[1], local_heads * head_width
    )
    partial_sum = jnp.dot(attended, out_weight, preferred_element_type=jnp.float32)
    return (normed, inverse, projected, attended, partial_sum)


def flatten(array):
    return array.reshape(-1, array.shape[-1])


def backward_local(
    cotangent, normed, projected, attended, gate, qk_gain, proj_weight, out_weight, temporal
):
    count_a, count_b = (cotangent.shape[0], cotangent.shape[1])
    scaled = (cotangent.astype(jnp.float32) * gate).astype(jnp.bfloat16)
    contract = (((0,), (0,)), ((), ()))
    grad_wout = lax.dot_general(
        flatten(attended), flatten(scaled), contract, preferred_element_type=jnp.float32
    )
    grad_att = lax.dot_general(
        scaled, out_weight, (((2,), (1,)), ((), ())), preferred_element_type=jnp.float32
    )
    grad_att = grad_att.astype(jnp.bfloat16).reshape(projected.shape[:3] + (projected.shape[4],))
    pullback = jax.vjp(partial(attend, qk_gain=qk_gain, temporal=temporal), projected)[1]
    grad_projected = pullback(grad_att)[0].astype(jnp.bfloat16).reshape(count_a, count_b, -1)
    grad_wproj = lax.dot_general(
        flatten(normed), flatten(grad_projected), contract, preferred_element_type=jnp.float32
    )
    grad_normed = lax.dot_general(
        grad_projected, proj_weight, (((2,), (1,)), ((), ())), preferred_element_type=jnp.float32
    )
    return (grad_normed, grad_wproj, grad_wout)


def finish(inputs, cotangent, summed, inverse, gain):
    widened = inputs.astype(jnp.float32)
    weighted = summed * gain
    grad_input = inverse * weighted - widened * inverse**3 * jnp.mean(
        widened * weighted, -1, keepdims=True
    )
    return (cotangent.astype(jnp.float32) + grad_input).astype(jnp.bfloat16)


def local(clip_tokens, out_cotangent, proj_weight, out_weight, norm_gain, branch_gate, qk_gain):
    full_proj, full_out = (
        lax.all_gather(proj_weight, "seq", axis=1, tiled=True),
        lax.all_gather(out_weight, "seq", axis=2, tiled=True),
    )
    normed_a, inverse_a, projected_a, attended_a, partial_a = forward_local(
        clip_tokens, norm_gain[0], qk_gain[0], full_proj[0], full_out[0], False
    )
    summed_a = lax.psum(partial_a.astype(jnp.bfloat16), "fsdp").astype(jnp.float32)
    middle_frames = (clip_tokens.astype(jnp.float32) + branch_gate[0] * summed_a).astype(
        jnp.bfloat16
    )
    middle = lax.all_to_all(middle_frames, "seq", split_axis=1, concat_axis=0, tiled=True)
    normed_b, inverse_b, projected_b, attended_b, partial_b = forward_local(
        middle, norm_gain[1], qk_gain[1], full_proj[1], full_out[1], True
    )
    summed_b = lax.psum(partial_b.astype(jnp.bfloat16), "fsdp").astype(jnp.float32)
    mixed_out = (middle.astype(jnp.float32) + branch_gate[1] * summed_b).astype(jnp.bfloat16)
    back_b, proj_late, outw_late = backward_local(
        out_cotangent,
        normed_b,
        projected_b,
        attended_b,
        branch_gate[1],
        qk_gain[1],
        full_proj[1],
        full_out[1],
        True,
    )
    summed_back_b = lax.psum(back_b.astype(jnp.bfloat16), "fsdp").astype(jnp.float32)
    grad_middle = finish(middle, out_cotangent, summed_back_b, inverse_b, norm_gain[1])
    grad_frames = lax.all_to_all(grad_middle, "seq", split_axis=0, concat_axis=1, tiled=True)
    back_a, proj_early, outw_early = backward_local(
        grad_frames,
        normed_a,
        projected_a,
        attended_a,
        branch_gate[0],
        qk_gain[0],
        full_proj[0],
        full_out[0],
        False,
    )
    summed_back_a = lax.psum(back_a.astype(jnp.bfloat16), "fsdp").astype(jnp.float32)
    grad_clip = finish(clip_tokens, grad_frames, summed_back_a, inverse_a, norm_gain[0])
    grad_proj, grad_outw = (
        lax.psum_scatter(
            jnp.stack([proj_early, proj_late]).astype(jnp.bfloat16),
            "seq",
            scatter_dimension=1,
            tiled=True,
        ).astype(jnp.float32),
        lax.psum_scatter(
            jnp.stack([outw_early, outw_late]).astype(jnp.bfloat16),
            "seq",
            scatter_dimension=2,
            tiled=True,
        ).astype(jnp.float32),
    )
    return (mixed_out, grad_clip, grad_proj.astype(jnp.bfloat16), grad_outw.astype(jnp.bfloat16))


def solution(mesh):
    placed = (
        P("seq", None, None),
        P(None, "seq", None),
        P(None, "seq", "fsdp"),
        P(None, "fsdp", "seq"),
        P(),
        P(),
        P(),
    )
    return jax.shard_map(
        local,
        mesh=mesh,
        in_specs=placed,
        out_specs=(
            P(None, "seq", None),
            P("seq", None, None),
            P(None, "seq", "fsdp"),
            P(None, "fsdp", "seq"),
        ),
        check_vma=False,
    )
```

profile of v0, /device:TPU:8, one launch (start us, length us, event | category | flops | bytes accessed | tf_op | source)
XLA Modules:
  0.0 927.6 jit_solution(13544255808152746060)
XLA Ops:
  14.6 34.3 %all-gather.5.cloned.1.call-done = bf16[2,256,3584]{1,0,2:T(2,128)(2,1)} async-done(((bf16[2,256,224]{1,0,2:T(2,128)(2,1)}), bf16[2,256,3584]{1,0,2:T(2,128)(2,1)}) %all-gather.5.cloned.1.call-update) | async-done | bytes 3670032 | tf_op jit(solution)/shard_map/all_gather | solution.py:91
  49.0 8.9 fusion.156
  57.9 8.6 copy.228
  66.5 49.0 %all-gather.3.cloned.1.call-done = bf16[2,3584,768]{2,1,0:T(8,128)(2,1)} async-done(((bf16[2,224,768]{2,1,0:T(8,128)(2,1)}), bf16[2,3584,768]{2,1,0:T(8,128)(2,1)}) %all-gather.3.cloned.1.call-update) | async-done | bytes 11010064 | tf_op jit(solution)/shard_map/all_gather | solution.py:90
  115.5 8.9 slice_bitcast_fusion
  124.4 8.3 copy.173
  143.1 101.4 %all-reduce.13.cloned.1.call-done = bf16[1,256,3584]{2,1,0:T(8,128)(2,1)} async-done(((bf16[1,256,3584]{2,1,0:T(8,128)(2,1)}), bf16[1,256,3584]{2,1,0:T(8,128)(2,1)}) %all-reduce.13.cloned.1.call-update) | async-done | bytes 1835024 | tf_op jit(solution)/shard_map/psum | solution.py:96
  246.6 4.6 copy.348
  251.7 13.1 %reduce.21 = bf16[256,3584]{1,0:T(8,128)(2,1)} reduce(bf16[256,1,3584]{2,1,0:T(2,128)(2,1)} %bitcast.270, bf16[]{:T(256)} %broadcast.418), dimensions={1}, to_apply=%bitcast.261.reduce_sub_computation | reduce | bytes 3670018
  264.8 5.4 reshape.505
  270.2 5.7 all-to-all-start
  279.6 8.5 copy.230
  291.4 8.2 copy.182
  300.4 10.2 %reshape.506 = bf16[256,1,3584]{2,1,0:T(2,128)(2,1)} reshape(bf16[16,2,28672]{2,1,0:T(2,128)(2,1)} %all-to-all-done) | data formatting | bytes 3670016
  339.4 5.6 fusion.11
  349.3 94.7 %all-reduce.15.cloned.1.call-done = bf16[16,16,3584]{2,1,0:T(8,128)(2,1)} async-done(((bf16[16,16,3584]{2,1,0:T(8,128)(2,1)}), bf16[16,16,3584]{2,1,0:T(8,128)(2,1)}) %all-reduce.15.cloned.1.call-update) | async-done | bytes 1835024 | tf_op jit(solution)/shard_map/psum | solution.py:117
  452.5 5.9 all-to-all-start.1
  465.0 17.9 %all-to-all-done.1 = bf16[16,16,3584]{2,1,0:T(8,128)(2,1)} async-done(((bf16[16,16,3584]{2,1,0:T(8,128)(2,1)}), bf16[16,16,3584]{2,1,0:T(8,128)(2,1)}, u32[]{:S(2)}, u32[]{:S(2)}) %all-to-all-start.1) | async-done | bytes 1835040 | tf_op jit(solution)/shard_map/all_to_all | solution.py:119
  489.0 9.9 %copy.214 = bf16[2,256,3584]{1,0,2:T(2,128)(2,1)} copy(bf16[2,256,3584]{2,1,0:T(8,128)(2,1)} %pad_maximum_fusion.1) | data formatting | bytes 7340032 | tf_op jit(solution)/shard_map/stack | solution.py:141
  514.5 5.5 fusion.17
  525.6 4.9 pad_maximum_fusion
  536.2 86.6 %all-reduce.17.cloned.1.call-done = bf16[2,256,3584]{1,0,2:T(2,128)(2,1)} async-done(((bf16[2,256,3584]{1,0,2:T(2,128)(2,1)}), bf16[2,256,3584]{1,0,2:T(2,128)(2,1)}) %all-reduce.17.cloned.1.call-update) | async-done | bytes 3670032
  624.6 170.6 %all-reduce.19.cloned.1.call-done = (bf16[16,16,3584]{2,1,0:T(8,128)(2,1)}, bf16[1,256,3584]{2,1,0:T(8,128)(2,1)}) async-done(((bf16[16,16,3584]{2,1,0:T(8,128)(2,1)}, bf16[1,256,3584]{2,1,0:T(8,128)(2,1)}), (bf16[16,16,3584]{2,1,0:T(8,128)(2,1)}, bf16[1,256,3584]{2,1,0:T(8,128)(2,1)})) %all-reduce.19.cloned.1.call-update) | async-done | bytes 3670032 | tf_op jit(solution)/shard_map/psum | solution.py:104
  803.8 116.8 %reduce-scatter.2.cloned.1.call-done = bf16[2,224,768]{2,1,0:T(8,128)(2,1)} async-done(((bf16[2,3584,768]{2,1,0:T(8,128)(2,1)}), bf16[2,224,768]{2,1,0:T(8,128)(2,1)}) %reduce-scatter.2.cloned.1.call-update) | async-done | bytes 688144 | tf_op jit(solution)/shard_map/reduce_scatter | solution.py:134
  (210 shorter events, 118.5 us)
Async XLA Ops:
  7.2 41.8 %all-gather.5.cloned.1.call-start = ((), (), s32[]{:S(2)}) async-start(), calls=%async_computation.4 | async-start | bytes 3899392 | tf_op jit(solution)/shard_map/all_gather | solution.py:91
  9.1 106.4 %all-gather.3.cloned.1.call-start = ((), (), s32[]{:S(2)}) async-start(), calls=%async_computation.3 | async-start | bytes 11698176 | tf_op jit(solution)/shard_map/all_gather | solution.py:90
  9.9 234.7 %all-reduce.13.cloned.1.call-start = ((), (), s32[]{:S(2)}) async-start(), calls=%async_computation.5 | async-start | bytes 3670016 | tf_op jit(solution)/shard_map/psum | solution.py:96
  10.8 121.9 %copy-start.19 = (f32[3584]{0:T(1024)}, f32[3584]{0:T(1024)S(1)}, u32[]{:S(2)}) copy-start(f32[3584]{0:T(1024)S(1)} %get-tuple-element.39) | copy-start | bytes 43012
  13.4 119.3 %copy-start.49 = (f32[256]{0:T(256)}, f32[256]{0:T(256)S(1)}, u32[]{:S(2)}) copy-start(f32[256]{0:T(256)S(1)} %get-tuple-element.59) | copy-start | bytes 3076
  14.6 123.0 %copy-start.51 = (f32[128]{0:T(128)}, f32[128]{0:T(128)S(1)}, u32[]{:S(2)}) copy-start(f32[128]{0:T(128)S(1)} %get-tuple-element.55) | copy-start | bytes 1540
  14.6 123.0 %copy-start.52 = (f32[128]{0:T(128)}, f32[128]{0:T(128)S(1)}, u32[]{:S(2)}) copy-start(f32[128]{0:T(128)S(1)} %get-tuple-element.56) | copy-start | bytes 1540
  124.4 8.3 copy-start.3
  139.5 107.1 %copy-start.16 = (bf16[2,128,256]{2,1,0:T(8,128)(2,1)}, bf16[2,128,256]{2,1,0:T(8,128)(2,1)S(1)}, u32[]{:S(2)}) copy-start(bf16[2,128,256]{2,1,0:T(8,128)(2,1)S(1)} %convolution_convert_fusion.10) | copy-start | bytes 393220
  143.1 108.1 %copy-start.23 = (f32[3584]{0:T(1024)}, f32[3584]{0:T(1024)S(1)}, u32[]{:S(2)}) copy-start(f32[3584]{0:T(1024)S(1)} %get-tuple-element.37) | copy-start | bytes 43012
  143.1 133.4 %copy-start.21 = (f32[3584]{0:T(1024)}, f32[3584]{0:T(1024)S(1)}, u32[]{:S(2)}) copy-start(f32[3584]{0:T(1024)S(1)} %get-tuple-element.36) | copy-start | bytes 43012
  270.2 30.2 %all-to-all-start = ((bf16[16,2,28672]{2,1,0:T(2,128)(2,1)}), bf16[16,2,28672]{2,1,0:T(2,128)(2,1)}, u32[]{:S(2)}, u32[]{:S(2)}) async-start(bf16[16,2,28672]{2,1,0:T(2,128)(2,1)} %reshape.505), calls=%async_computation | async-start | bytes 3670016 | tf_op jit(solution)/shard_map/all_to_all | solution.py:100
  275.9 168.1 %all-reduce.15.cloned.1.call-start = ((), (), s32[]{:S(2)}) async-start(), calls=%async_computation.6 | async-start | bytes 3670016 | tf_op jit(solution)/shard_map/psum | solution.py:117
  318.6 10.6 %copy-start.13 = (bf16[16,16,2,128]{3,1,2,0:T(8,128)(2,1)}, bf16[16,16,2,128]{3,1,2,0:T(8,128)(2,1)S(1)}, u32[]{:S(2)}) copy-start(bf16[16,16,2,128]{3,1,2,0:T(8,128)(2,1)S(1)} %fusion.86) | copy-start | bytes 393220
  452.5 6.1 copy-start.14
  452.5 6.1 copy-start.29
  452.5 6.1 copy-start.30
  452.5 30.4 %all-to-all-start.1 = ((bf16[16,16,3584]{2,1,0:T(8,128)(2,1)}), bf16[16,16,3584]{2,1,0:T(8,128)(2,1)}, u32[]{:S(2)}, u32[]{:S(2)}) async-start(bf16[16,16,3584]{2,1,0:T(8,128)(2,1)} %fusion.23), calls=%async_computation.1 | async-start | bytes 3670016 | tf_op jit(solution)/shard_map/all_to_all | solution.py:119
  458.4 24.5 %copy-start.24 = (f32[3584]{0:T(1024)S(1)}, f32[3584]{0:T(1024)}, u32[]{:S(2)}) copy-start(f32[3584]{0:T(1024)} %copy-done.23) | copy-start | bytes 43012
  458.4 164.4 %all-reduce.17.cloned.1.call-start = ((), (), s32[]{:S(2)}) async-start(), calls=%async_computation.8 | async-start | bytes 7340032
  461.5 24.7 %copy-start.17 = (bf16[2,128,256]{2,1,0:T(8,128)(2,1)S(1)}, bf16[2,128,256]{2,1,0:T(8,128)(2,1)}, u32[]{:S(2)}) copy-start(bf16[2,128,256]{2,1,0:T(8,128)(2,1)} %copy-done.16) | copy-start | bytes 393220
  498.9 296.3 %all-reduce.19.cloned.1.call-start = ((), (), s32[]{:S(2)}) async-start(), calls=%async_computation.9 | async-start | bytes 7340032 | tf_op jit(solution)/shard_map/psum | solution.py:104
  520.0 400.6 %reduce-scatter.2.cloned.1.call-start = ((), (), s32[]{:S(2)}) async-start(), calls=%async_computation.7 | async-start | bytes 11698176 | tf_op jit(solution)/shard_map/reduce_scatter | solution.py:134
  536.2 261.3 %copy-start.22 = (f32[3584]{0:T(1024)S(1)}, f32[3584]{0:T(1024)}, u32[]{:S(2)}) copy-start(f32[3584]{0:T(1024)} %copy-done.21) | copy-start | bytes 43012
  (41 other events, 135.5 us)
Sparse Core Ops, SparseCore 0:
  10.3 38.6 all-gather.4
  50.6 64.7 all-gather.2
  143.1 101.4 all-reduce.12
  345.2 98.8 all-reduce.14
  499.0 123.7 all-reduce.16
  625.8 169.3 all-reduce.18
  798.2 122.3 reduce-scatter.1
where the time goes:
time: 941 us; the launch traced here: 928 us
  waiting for transfers between devices  673 us (72%)
  local copies, waits for them, and re-layouts  102 us (11%)
  other arithmetic  67.5 us (7%)
  matrix products  57.4 us (6%)
  between operations  15.7 us (2%)
  starting transfers between devices  12.7 us (1%)
    psum x1, waiting for transfers between devices, local(): lax.psum(partial_b.astype(jnp.bfloat16), 'fsdp').astype(jnp.float32)  171 us
    reduce_scatter x1, waiting for transfers between devices, local(): lax.psum_scatter(jnp.stack([proj_early, proj_late]).astype(jnp.bfloat16),...  117 us
    psum x1, waiting for transfers between devices, local(): lax.psum(partial_a.astype(jnp.bfloat16), 'fsdp').astype(jnp.float32)  101 us
    psum x1, waiting for transfers between devices, local(): lax.psum(back_b.astype(jnp.bfloat16), 'fsdp').astype(jnp.float32)  94.7 us
    unnamed x8, waiting for transfers between devices  87.4 us
    all_gather x1, waiting for transfers between devices, local(): lax.all_gather(proj_weight, 'seq', axis=1, tiled=True)  49 us
    unnamed x121, local copies, waits for them, and re-layouts  45.7 us
    all_gather x1, waiting for transfers between devices, local(): lax.all_gather(out_weight, 'seq', axis=2, tiled=True)  34.3 us
  transfers between devices with their start and end apart: 9, of which 9 were waited for; matrix products, arithmetic and copies ran while one was open for 11% of the time, Pallas kernels for 0%

commit v1 on v0

v1 whole, which is shorter than its diff:
```python
import functools

import jax
import jax.numpy as jnp
from jax import lax
from jax.experimental import pallas as pl
from jax.experimental.pallas import tpu as pltpu
from jax.sharding import PartitionSpec as P

EPS = 1e-06
MESH = pl.DeviceIdType.MESH
D = 3584
HD = 128
T = 256
OWN = 32
GROUP = 896
SH = 224
WC = 1024
PC = 768
TILE = 512
NT = D // TILE
F32 = jnp.float32
BF16 = jnp.bfloat16
VMEM_LIMIT = 60 * 1024 * 1024


def tile_at(i, size=TILE):
    return pl.ds(pl.multiple_of(i * size, size), size)


def dot(a, b, contract=((1,), (0,))):
    return lax.dot_general(a, b, (contract, ((), ())), preferred_element_type=F32)


def head_forward(proj_ref, qkg, head, temporal):
    base = head * 3 * HD
    q_raw = proj_ref[:, base : base + HD]
    k_raw = proj_ref[:, base + HD : base + 2 * HD]
    q_inv = lax.rsqrt(jnp.mean(q_raw * q_raw, -1, keepdims=True) + EPS)
    k_inv = lax.rsqrt(jnp.mean(k_raw * k_raw, -1, keepdims=True) + EPS)
    q = (q_raw * q_inv * qkg[0:1, :]).astype(BF16)
    k = (k_raw * k_inv * qkg[1:2, :]).astype(BF16)
    v = proj_ref[:, base + 2 * HD : base + 3 * HD].astype(BF16)
    scores = dot(q, k, ((1,), (1,))) * HD**-0.5
    if temporal:
        rows = lax.broadcasted_iota(jnp.int32, (T, T), 0)
        cols = lax.broadcasted_iota(jnp.int32, (T, T), 1)
        scores = jnp.where((rows & 15) == (cols & 15), scores, -1e30)
    top = jnp.max(scores, -1, keepdims=True)
    grown = jnp.exp(scores - top)
    probs = grown / jnp.sum(grown, -1, keepdims=True)
    return q_raw, k_raw, q_inv, k_inv, q, k, v, probs


def head_backward(proj_ref, qkg, head, temporal, d_att, dproj_ref):
    q_raw, k_raw, q_inv, k_inv, q, k, v, probs = head_forward(proj_ref, qkg, head, temporal)
    base = head * 3 * HD
    rounded = probs.astype(BF16)
    d_probs = dot(d_att, v, ((1,), (1,))).astype(BF16).astype(F32)
    d_v = dot(rounded, d_att, ((0,), (0,)))
    d_scores = probs * (d_probs - jnp.sum(probs * d_probs, -1, keepdims=True))
    d_scores = (d_scores * HD**-0.5).astype(BF16)
    d_q = dot(d_scores, k).astype(BF16).astype(F32) * qkg[0:1, :]
    d_k = dot(d_scores, q, ((0,), (0,))).astype(BF16).astype(F32) * qkg[1:2, :]
    d_q = q_inv * d_q - q_raw * (q_inv * q_inv * q_inv) * jnp.mean(q_raw * d_q, -1, keepdims=True)
    d_k = k_inv * d_k - k_raw * (k_inv * k_inv * k_inv) * jnp.mean(k_raw * d_k, -1, keepdims=True)
    dproj_ref[:, base : base + HD] = d_q.astype(BF16)
    dproj_ref[:, base + HD : base + 2 * HD] = d_k.astype(BF16)
    dproj_ref[:, base + 2 * HD : base + 3 * HD] = d_v.astype(BF16)


def inverse_norm(x_ref):
    def square(i, total):
        x = x_ref[:, tile_at(i)].astype(F32)
        return total + jnp.sum(x * x, -1, keepdims=True)

    total = lax.fori_loop(0, NT, square, jnp.zeros((T, 1), F32))
    return lax.rsqrt(total / D + EPS)


def normalise(x_ref, gain, normed_ref):
    inverse = inverse_norm(x_ref)

    @pl.loop(0, NT)
    def _(i):
        at = tile_at(i)
        normed_ref[:, at] = (x_ref[:, at].astype(F32) * inverse * gain[:, at]).astype(BF16)


def project(group, normed_ref, w_ref, proj_ref, first):
    at = tile_at(group, GROUP)
    product = dot(normed_ref[:, at], w_ref[at, :PC])
    if first:
        proj_ref[...] = product
    else:
        proj_ref[...] += product


def branch(proj_ref, qkg, w_ref, att_ref, part_ref, temporal):
    for head in range(2):
        parts = head_forward(proj_ref, qkg, head, temporal)
        att_ref[:, head * HD : (head + 1) * HD] = dot(parts[7].astype(BF16), parts[6]).astype(BF16)
    att = att_ref[...]

    @pl.loop(0, NT)
    def _(i):
        at = tile_at(i)
        part_ref[:, at] = dot(att, w_ref[at, PC:], ((1,), (1,))).astype(BF16)


def scaled_tile(dy_ref, gate, at):
    return (dy_ref[:, at].astype(F32) * gate[:, at]).astype(BF16)


def backward(dy_ref, w_ref, gate, qkg, proj_ref, dpart_ref, datt_ref, dproj_ref, temporal):
    datt_ref[...] = jnp.zeros_like(datt_ref)

    @pl.loop(0, NT)
    def _(i):
        at = tile_at(i)
        datt_ref[...] += dot(scaled_tile(dy_ref, gate, at), w_ref[at, PC:])

    for head in range(2):
        d_att = datt_ref[:, head * HD : (head + 1) * HD].astype(BF16)
        head_backward(proj_ref, qkg, head, temporal, d_att, dproj_ref)
    dproj = dproj_ref[...]

    @pl.loop(0, NT)
    def _(i):
        at = tile_at(i)
        dpart_ref[:, at] = dot(dproj, w_ref[at, :PC], ((1,), (1,))).astype(BF16)


def weight_grads(dy_ref, gate, normed_ref, att_ref, dproj_ref, g_ref):
    dproj = dproj_ref[...]
    att = att_ref[...]

    @pl.loop(0, NT)
    def _(i):
        at = tile_at(i)
        g_ref[at, :PC] = dot(normed_ref[:, at], dproj, ((0,), (0,))).astype(BF16)
        g_ref[at, PC:] = dot(scaled_tile(dy_ref, gate, at), att, ((0,), (0,))).astype(BF16)


def place():
    return lax.axis_index("seq"), lax.axis_index("fsdp")


def remote(src, dst, send, recv, device):
    return pltpu.make_async_remote_copy(
        src_ref=src, dst_ref=dst, send_sem=send, recv_sem=recv, device_id=device, device_id_type=MESH
    )


def sibling():
    s, f = place()
    return (s + 1 - 2 * lax.rem(s, 2), f)


def seq_node(dp, dq):
    s, f = place()
    node = 2 * lax.rem(s // 4 + dp + 4, 4) + lax.rem(s // 2 + dq, 2)
    s_there = 2 * node + lax.rem(s, 2)
    return (s_there, f), s_there * SH


def fsdp_node(dp, dq):
    s, f = place()
    return (s, 2 * lax.rem(f // 2 + dp + 4, 4) + lax.rem(f + dq, 2))


def by_frames(dp, dq):
    device = fsdp_node(dp, dq)
    return device, device[1] * OWN


def by_positions(dp, dq):
    s, _ = place()
    device = fsdp_node(dp, dq)
    shifted = 2 * lax.rem(device[1] // 2 + s // 4, 4) + lax.rem(device[1], 2)
    return device, shifted * OWN


def swap_out():
    s, _ = place()
    pair = by_positions(0, 0)[1] // OWN
    return [(2 * pair + e, s // 2) for e in range(2)]


def swap_back():
    s, f = place()
    there = 2 * lax.rem(s // 4 - f // 2 + 4, 4) + lax.rem(s // 2, 2)
    return [(2 * f + i, there) for i in range(2)]


def is_me(device):
    s, f = place()
    return jnp.logical_and(device[0] == s, device[1] == f)


def greet():
    barrier = pltpu.get_barrier_semaphore()
    peers = [sibling()]
    for dp, dq in ((1, 0), (-1, 0), (0, 1)):
        peers += [seq_node(dp, dq)[0], fsdp_node(dp, dq)]
    for peer in peers:
        pl.semaphore_signal(barrier, inc=1, device_id=peer, device_id_type=MESH)
    count = len(peers)
    for peer in swap_out() + swap_back():
        other = jnp.logical_not(is_me(peer))
        count = count + other.astype(jnp.int32)

        @pl.when(other)
        def _():
            pl.semaphore_signal(barrier, inc=1, device_id=peer, device_id_type=MESH)

    pl.semaphore_wait(barrier, count)


def rows_at(start, n):
    return pl.ds(pl.multiple_of(start, 16), n)


class Gather:
    MESSAGES = (
        ((0, 0), None, (1, 0)),
        ((0, 0), None, (-1, 0)),
        ((0, 0), None, (0, 1)),
        ((-1, 0), 0, (1, 0)),
        ((1, 0), 1, (-1, 0)),
        ((0, 1), None, (1, 0)),
        ((0, 1), None, (-1, 0)),
        ((2, 0), 0, (0, 1)),
        ((2, 0), 1, (0, 1)),
    )

    def __init__(self, ref, node, size, sems):
        self.ref, self.node, self.size, self.sems = ref, node, size, sems

    def copy(self, m):
        shard, half, target = self.MESSAGES[m]
        start, n = self.node(*shard)[1], self.size
        if half is not None:
            n = n // 2
            start = start + half * n
        rows = self.ref.at[rows_at(start, n)]
        return remote(rows, rows, self.sems.at[0, m], self.sems.at[1, m], self.node(*target)[0])

    def send(self, *messages):
        for m in messages:
            self.copy(m).start()

    def got(self, *messages):
        for m in messages:
            self.copy(m).wait_recv()

    def start(self):
        self.send(0, 1, 2)

    def middle(self):
        self.got(0)
        self.send(3)
        self.got(1)
        self.send(4)
        self.got(2)
        self.send(5, 6)

    def last(self):
        self.got(3)
        self.send(7)
        self.got(4)
        self.send(8)

    def end(self):
        self.got(5, 6, 7, 8)
        self.sent()

    def sent(self):
        for m in range(9):
            self.copy(m).wait_send()


class Weights(Gather):
    SHARDS = ((0, 0), (-1, 0), (1, 0), (0, 1), (2, 0), (-1, 1), (1, 1), (2, 1))

    def __init__(self, block, proj_ref, outw_ref, w_ref, sems, near_sems, local):
        super().__init__(w_ref, seq_node, SH, sems)
        self.near_sems = near_sems
        rows = rows_at(seq_node(0, 0)[1], SH)
        self.own = [
            pltpu.make_async_copy(proj_ref.at[block], w_ref.at[rows, pl.ds(0, PC)], local.at[0]),
            pltpu.make_async_copy(outw_ref.at[block], w_ref.at[rows, pl.ds(PC, WC - PC)], local.at[1]),
        ]

    def near(self, n):
        rows = self.ref.at[rows_at(self.node(*self.SHARDS[n])[1], SH)]
        return remote(rows, rows, self.near_sems.at[0, n], self.near_sems.at[1, n], sibling())

    def near_got(self, *shards):
        for n in shards:
            self.near(n).wait_recv()

    def load(self):
        for copy in self.own:
            copy.start()

    def start(self):
        for copy in self.own:
            copy.wait()
        super().start()
        self.near(0).start()

    def middle(self):
        self.got(0)
        self.send(3)
        self.near(1).start()
        self.got(1)
        self.send(4)
        self.near(2).start()
        self.got(2)
        self.send(5, 6)
        self.near(3).start()

    def last(self):
        super().last()
        self.near(4).start()

    def fifth(self):
        self.got(5)
        self.near(5).start()
        self.got(6)
        self.near(6).start()

    def end(self):
        self.got(7, 8)
        self.near(7).start()

    def sent(self):
        super().sent()
        for n in range(8):
            self.near(n).wait_send()


def add_rows(ref, start, n, stage):
    @pl.loop(0, n // 16)
    def _(i):
        rows, here = rows_at(start + i * 16, 16), rows_at(i * 16, 16)
        ref[rows, :] = (ref[rows, :].astype(F32) + stage[here, :].astype(F32)).astype(BF16)


class Reduce:
    MESSAGES = (
        ((-1, 0), None, (-1, 0), 5),
        ((1, 0), None, (1, 0), 6),
        ((0, 1), None, (0, 1), 4),
        ((2, 0), 0, (-1, 0), 3),
        ((2, 0), 1, (1, 0), 3),
        ((-1, 1), None, (-1, 0), 1),
        ((1, 1), None, (1, 0), 2),
        ((2, 1), None, (0, 1), 0),
    )

    def __init__(self, ref, node, size, held, sems):
        self.ref, self.node, self.size, self.held, self.sems = ref, node, size, held, sems

    def copy(self, m):
        shard, half, target, slot = self.MESSAGES[m]
        start, n, first = self.node(*shard)[1], self.size, 0
        if half is not None:
            n = n // 2
            first = half * n
        src = self.ref.at[rows_at(start + first, n)]
        dst = self.held.at[pl.ds(slot * self.size + first, n)]
        return remote(src, dst, self.sems.at[0, m], self.sems.at[1, m], self.node(*target)[0])

    def send(self, *messages):
        for m in messages:
            self.copy(m).start()

    def got(self, *messages):
        for m in messages:
            self.copy(m).wait_recv()

    def add(self, shard, slot, half=None):
        start, n, first = self.node(*shard)[1], self.size, 0
        if half is not None:
            n = n // 2
            first = half * n
        add_rows(self.ref, start + first, n, self.held.at[pl.ds(slot * self.size + first, n)])

    def ready(self, *shards):
        pass

    def start(self):
        self.ready(0, 1, 2)
        self.send(7, 5, 6)

    def middle(self):
        self.ready(3)
        self.got(7)
        self.add((2, 0), 0)
        self.send(3, 4)
        self.ready(4)
        self.got(5)
        self.add((0, 1), 1)
        self.got(6)
        self.add((0, 1), 2)
        self.send(2)

    def last(self):
        self.ready(5)
        self.got(3)
        self.add((-1, 0), 3, 0)
        self.send(0)
        self.ready(6)
        self.got(4)
        self.add((1, 0), 3, 1)
        self.send(1)

    def end(self):
        self.ready(7)
        self.got(0, 1, 2)
        for m in range(8):
            self.copy(m).wait_send()

    def total(self, at):
        summed = self.ref[rows_at(self.node(0, 0)[1], self.size), at].astype(F32)
        for slot in (4, 5, 6):
            summed = summed + self.held[pl.ds(slot * self.size, self.size), at].astype(F32)
        return summed


class WeightGrads(Reduce):
    SHARDS = ((2, 1), (-1, 1), (1, 1), (2, 0), (0, 1), (-1, 0), (1, 0), (0, 0))

    def __init__(self, ref, held, sems, near_held, near_sems):
        super().__init__(ref, seq_node, SH, held, sems)
        self.near_held, self.near_sems = near_held, near_sems

    def near(self, n):
        s, _ = place()
        start = self.node(*self.SHARDS[n])[1] + (1 - 2 * lax.rem(s, 2)) * SH
        return remote(
            self.ref.at[rows_at(start, SH)], self.near_held.at[pl.ds(n * SH, SH)],
            self.near_sems.at[0, n], self.near_sems.at[1, n], sibling(),
        )

    def ready(self, *shards):
        for n in shards:
            self.near(n).wait_recv()
            add_rows(self.ref, self.node(*self.SHARDS[n])[1], SH, self.near_held.at[pl.ds(n * SH, SH)])

    def pair(self):
        for n in range(8):
            self.near(n).start()

    def result(self, block, gproj_ref, goutw_ref):
        base = self.node(0, 0)[1]

        @pl.loop(0, SH // 16)
        def _(i):
            rows, here = rows_at(base + i * 16, 16), rows_at(i * 16, 16)
            total = self.ref[rows, :].astype(F32)
            for slot in (4, 5, 6):
                total = total + self.held[rows_at(slot * SH + i * 16, 16), :].astype(F32)
            gproj_ref[block, here, :] = total[:, :PC].astype(BF16)
            goutw_ref[block, here, :] = total[:, PC:].astype(BF16)

        for n in range(8):
            self.near(n).wait_send()


class Swap:
    def __init__(self, src_ref, dst_ref, targets, sources, base, sems, local):
        self.src_ref, self.dst_ref, self.targets, self.base = src_ref, dst_ref, targets, base
        self.sources, self.sems, self.local = sources, sems, local

    def each(self, act):
        s, _ = place()
        for j in range(2):
            src = self.src_ref.at[pl.ds(j * 16, 16)]
            there = self.dst_ref.at[rows_at(s * 16, 16)]
            here = self.dst_ref.at[rows_at(self.base + j * 16, 16)]
            act(j, src, there, here)

    def start(self):
        s, _ = place()

        def act(j, src, there, here):
            mine = is_me(self.targets[j])

            @pl.when(mine)
            def _():
                pltpu.make_async_copy(src, here, self.local).start()

            @pl.when(jnp.logical_not(mine))
            def _():
                remote(src, there, self.sems.at[0, j], self.sems.at[1, lax.rem(s, 2)], self.targets[j]).start()

        self.each(act)

    def wait(self):
        def act(j, src, there, here):
            mine = is_me(self.targets[j])
            copy = lambda: remote(src, here, self.sems.at[0, j], self.sems.at[1, j], self.targets[j])

            @pl.when(mine)
            def _():
                pltpu.make_async_copy(src, here, self.local).wait()

            @pl.when(jnp.logical_not(mine))
            def _():
                copy().wait_send()
                copy().wait_recv()

        self.each(act)


def branch_end(x_ref, x_base, gate, reduced, out_ref):
    @pl.loop(0, NT)
    def _(i):
        at = tile_at(i)
        value = x_ref[rows_at(x_base, OWN), at].astype(F32) + gate[:, at] * reduced.total(at)
        out_ref[:, at] = value.astype(BF16)


def input_grad(x_ref, x_base, dy_ref, dy_base, gain, reduced, sum_ref, out_ref):
    def moments(i, carry):
        squares, cross = carry
        at = tile_at(i)
        x = x_ref[rows_at(x_base, OWN), at].astype(F32)
        weighted = reduced.total(at) * gain[:, at]
        sum_ref[:, at] = weighted
        return squares + jnp.sum(x * x, -1, keepdims=True), cross + jnp.sum(x * weighted, -1, keepdims=True)

    zero = jnp.zeros((OWN, 1), F32)
    squares, cross = lax.fori_loop(0, NT, moments, (zero, zero))
    inverse = lax.rsqrt(squares / D + EPS)
    factor = inverse * inverse * inverse * (cross / D)

    @pl.loop(0, NT)
    def _(i):
        at = tile_at(i)
        x = x_ref[rows_at(x_base, OWN), at].astype(F32)
        value = dy_ref[rows_at(dy_base, OWN), at].astype(F32) + (inverse * sum_ref[:, at] - x * factor)
        out_ref[:, at] = value.astype(BF16)


def whole(
    x_ref, dy_ref, proj_in, outw_in, gain_ref, gate_ref, qkg_ref,
    mixed_ref, clip_ref, gproj_ref, goutw_ref,
    w0_ref, w1_ref, g_ref, normed0_ref, normed1_ref, proj0_ref, proj1_ref, att0_ref, att1_ref, datt_ref, dproj_ref,
    part_ref, part1_ref, middle_ref, grad_ref, held_ref, own_ref, sum_ref, near1_ref, far1_ref,
    w_sems, wn_sems, local, rs_sems, ag_sems, g_sems, gn_sems, swap_sems,
):
    s, f = place()
    x_group = s // 4
    gain0, gain1, gate0, gate1 = (r.at[pl.ds(b, 1)] for r in (gain_ref, gate_ref) for b in range(2))
    qkg0, qkg1 = qkg_ref[0], qkg_ref[1]
    w0 = Weights(0, proj_in, outw_in, w0_ref, w_sems.at[0], wn_sems.at[0], local.at[0])
    w1 = Weights(1, proj_in, outw_in, w1_ref, w_sems.at[1], wn_sems.at[1], local.at[1])
    positions, frames = by_positions(0, 0)[1], by_frames(0, 0)[1]

    w0.load()
    w1.load()
    greet()
    w0.start()
    normalise(x_ref, gain0, normed0_ref)
    w0.middle()
    w0.near_got(0, 3)
    project(x_group, normed0_ref, w0_ref, proj0_ref, True)
    w0.last()
    w0.fifth()
    w1.start()
    w0.near_got(1, 5)
    project(lax.rem(x_group + 3, 4), normed0_ref, w0_ref, proj0_ref, False)
    w0.near_got(2, 6)
    project(lax.rem(x_group + 1, 4), normed0_ref, w0_ref, proj0_ref, False)
    w0.end()
    w0.near_got(4, 7)
    project(lax.rem(x_group + 2, 4), normed0_ref, w0_ref, proj0_ref, False)
    branch(proj0_ref, qkg0, w0_ref, att0_ref, part_ref, False)

    r0 = Reduce(part_ref, by_positions, OWN, held_ref.at[0], rs_sems.at[0])
    r0.start()
    w1.middle()
    r0.middle()
    r0.last()
    w1.last()
    r0.end()
    branch_end(x_ref, positions, gate0, r0, own_ref.at[0])
    out = Swap(own_ref.at[0], middle_ref, swap_out(), None, frames, swap_sems.at[0], local.at[2, 0])
    out.start()
    w1.fifth()
    out.wait()
    a0 = Gather(middle_ref, by_frames, OWN, ag_sems.at[0])
    a0.start()
    w1.end()
    a0.middle()
    a0.last()
    w0.sent()
    w1.sent()
    w1.near_got(0, 1, 2, 3, 4, 5, 6, 7)
    a0.end()

    normalise(middle_ref, gain1, normed1_ref)
    for group in range(4):
        project(group, normed1_ref, w1_ref, proj1_ref, group == 0)
    branch(proj1_ref, qkg1, w1_ref, att1_ref, part1_ref, True)
    r1 = Reduce(part1_ref, by_frames, OWN, held_ref.at[1], rs_sems.at[1])
    r1.start()
    backward(dy_ref, w1_ref, gate1, qkg1, proj1_ref, part_ref, datt_ref, dproj_ref, True)

    r2 = Reduce(part_ref, by_frames, OWN, held_ref.at[2], rs_sems.at[2])
    r2.start()
    r1.middle()
    weight_grads(dy_ref, gate1, normed1_ref, att1_ref, dproj_ref, g_ref)
    grads1 = WeightGrads(g_ref, far1_ref, g_sems.at[1], near1_ref, gn_sems.at[1])
    grads1.pair()
    r2.middle()
    r1.last()
    r2.last()
    grads1.start()
    r2.end()
    input_grad(middle_ref, frames, dy_ref, frames, gain1, r2, sum_ref, own_ref.at[1])
    back = Swap(own_ref.at[1], grad_ref, swap_back(), None, positions, swap_sems.at[1], local.at[2, 0])
    back.start()
    r1.end()
    branch_end(middle_ref, frames, gate1, r1, own_ref.at[2])
    keep = pltpu.make_async_copy(own_ref.at[2], mixed_ref.at[rows_at(frames, OWN)], local.at[2, 1])
    keep.start()
    back.wait()
    a1 = Gather(grad_ref, by_positions, OWN, ag_sems.at[1])
    a1.start()
    grads1.middle()
    a1.middle()
    grads1.last()
    a1.last()
    keep.wait()
    a2 = Gather(mixed_ref, by_frames, OWN, ag_sems.at[2])
    a2.start()
    grads1.end()
    grads1.result(1, gproj_ref, goutw_ref)
    a1.end()

    backward(grad_ref, w0_ref, gate0, qkg0, proj0_ref, part_ref, datt_ref, dproj_ref, False)
    r3 = Reduce(part_ref, by_positions, OWN, held_ref.at[3], rs_sems.at[3])
    r3.start()
    a2.middle()
    weight_grads(grad_ref, gate0, normed0_ref, att0_ref, dproj_ref, g_ref)
    near0_ref, far0_ref = w1_ref.at[pl.ds(0, 8 * SH)], w1_ref.at[pl.ds(8 * SH, 7 * SH)]
    grads0 = WeightGrads(g_ref, far0_ref, g_sems.at[0], near0_ref, gn_sems.at[0])
    grads0.pair()
    r3.middle()
    r3.last()
    grads0.start()
    a2.last()
    r3.end()
    input_grad(x_ref, positions, grad_ref, positions, gain0, r3, sum_ref, own_ref.at[3])
    keep = pltpu.make_async_copy(own_ref.at[3], clip_ref.at[rows_at(positions, OWN)], local.at[2, 1])
    keep.start()
    keep.wait()
    a3 = Gather(clip_ref, by_positions, OWN, ag_sems.at[3])
    a3.start()
    grads0.middle()
    a3.middle()
    grads0.last()
    a3.last()
    a2.end()
    grads0.end()
    grads0.result(0, gproj_ref, goutw_ref)
    a3.end()


def shaped(shape, dtype=BF16):
    return jax.ShapeDtypeStruct(shape, dtype)


def sem(*shape):
    return pltpu.SemaphoreType.DMA(shape)


def local_program(clip_tokens, out_cotangent, proj_weight, out_weight, norm_gain, branch_gate, qk_gain):
    in_vmem = pl.BlockSpec(memory_space=pltpu.VMEM)
    anywhere = pl.BlockSpec(memory_space=pl.ANY)
    tokens = lambda *lead: pltpu.VMEM((*lead, T, D), BF16)
    mixed, clip, gproj, goutw = pl.pallas_call(
        whole,
        out_shape=[shaped((T, D)), shaped((T, D)), shaped((2, SH, PC)), shaped((2, SH, WC - PC))],
        in_specs=[in_vmem, in_vmem, anywhere, anywhere, in_vmem, in_vmem, in_vmem],
        out_specs=[anywhere, anywhere, in_vmem, in_vmem],
        scratch_shapes=[
            pltpu.VMEM((D, WC), BF16),
            pltpu.VMEM((D, WC), BF16),
            pltpu.VMEM((D, WC), BF16),
            tokens(),
            tokens(),
            pltpu.VMEM((T, PC), F32),
            pltpu.VMEM((T, PC), F32),
            pltpu.VMEM((T, 2 * HD), BF16),
            pltpu.VMEM((T, 2 * HD), BF16),
            pltpu.VMEM((T, 2 * HD), F32),
            pltpu.VMEM((T, PC), BF16),
            tokens(),
            tokens(),
            tokens(),
            tokens(),
            pltpu.VMEM((4, 7 * OWN, D), BF16),
            pltpu.VMEM((4, OWN, D), BF16),
            pltpu.VMEM((OWN, D), F32),
            pltpu.VMEM((8 * SH, WC), BF16),
            pltpu.VMEM((7 * SH, WC), BF16),
            sem(2, 2, 9),
            sem(2, 2, 8),
            sem(3, 2),
            sem(4, 2, 8),
            sem(4, 2, 9),
            sem(2, 2, 8),
            sem(2, 2, 8),
            sem(2, 2, 2),
        ],
        compiler_params=pltpu.CompilerParams(
            vmem_limit_bytes=VMEM_LIMIT, collective_id=0, has_side_effects=True
        ),
        name="two_blocks",
    )(
        clip_tokens.reshape(T, D),
        out_cotangent.reshape(T, D),
        proj_weight,
        jnp.swapaxes(out_weight, 1, 2),
        norm_gain,
        branch_gate,
        qk_gain,
    )
    return mixed.reshape(16, 16, D), clip.reshape(1, T, D), gproj, jnp.swapaxes(goutw, 1, 2)


def solution(mesh):
    placed = (
        P("seq", None, None),
        P(None, "seq", None),
        P(None, "seq", "fsdp"),
        P(None, "fsdp", "seq"),
        P(),
        P(),
        P(),
    )
    return jax.shard_map(
        local_program,
        mesh=mesh,
        in_specs=placed,
        out_specs=(
            P(None, "seq", None),
            P("seq", None, None),
            P(None, "seq", "fsdp"),
            P(None, "fsdp", "seq"),
        ),
        check_vma=False,
    )
```

time: 941 us -> 243 us (0.26); the launches traced: 928 us -> 243 us
  waiting for transfers between devices: 673 us -> 0 us
  Pallas kernels: 0 us -> 236 us
  local copies, waits for them, and re-layouts: 102 us -> 6.09 us
  other arithmetic: 67.5 us -> 0 us
  matrix products: 57.4 us -> 0 us
  between operations: 15.7 us -> 0.65 us
  starting transfers between devices: 12.7 us -> 0 us
    psum x3 -> x0, waiting for transfers between devices: 367 us -> none  [the longest x1 171 us: local(): lax.psum(partial_b.astype(jnp.bfloat16), 'fsdp').astype(jnp.float32)]
    pallas_call x0 -> x1, Pallas kernels: none -> 236 us  [local_program(): pl.pallas_call(whole, out_shape=[shaped((T, D)), shaped((T, D)), shaped((...]
    reduce_scatter x1 -> x0, waiting for transfers between devices: 117 us -> none  [local(): lax.psum_scatter(jnp.stack([proj_early, proj_late]).astype(jnp.bfloat16),...]
    unnamed x8 -> x0, waiting for transfers between devices: 87.4 us -> none
    all_gather x2 -> x0, waiting for transfers between devices: 83.3 us -> none  [the longest x1 49 us: local(): lax.all_gather(proj_weight, 'seq', axis=1, tiled=True)]
    dot_general x22 -> x0, matrix products: 53.7 us -> none  [the longest x2 11.1 us: backward_local(): lax.dot_general(grad_projected, proj_weight, (((2,), (1,)), ((), ())), pr...]
    unnamed x121 -> x10, local copies, waits for them, and re-layouts: 45.7 us -> 6.09 us
    convert_element_type x13 -> x0, other arithmetic: 27.9 us -> none  [the longest x3 10.7 us: finish(): return (cotangent.astype(jnp.float32) + grad_input).astype(jnp.bfloat16)]
  transfers between devices with their start and end apart: 9 -> 0, of which waited for: 9 -> 0; matrix products, arithmetic and copies ran while one was open for 11% -> 0% of each run, Pallas kernels for 0% -> 0%
where the time goes in v1:
time: 243 us
  Pallas kernels  236 us (97%)
  local copies, waits for them, and re-layouts  6.09 us (3%)
    pallas_call x1, Pallas kernels, local_program(): pl.pallas_call(whole, out_shape=[shaped((T, D)), shaped((T, D)), shaped((...  236 us
    unnamed x10, local copies, waits for them, and re-layouts  6.09 us

profile of v1, /device:TPU:8, one launch (start us, length us, event | category | flops | bytes accessed | tf_op | source)
XLA Modules:
  0.0 242.9 jit_solution(14594015096076571838)
XLA Ops:
  0.6 236.2 %two_blocks.1 = (bf16[256,3584]{1,0:T(8,128)(2,1)}, bf16[256,3584]{1,0:T(8,128)(2,1)}, bf16[2,224,768]{2,1,0:T(8,128)(2,1)}, bf16[2,224,256]{2,1,0:T(8,128)(2,1)}) custom-call(bf16[256,3584]{1,0:T(8,128)(2,1)} %bitcast.8, bf16[256,3584]{1,0:T(8,128)(2,1)} %bitcast.9, bf16[2,224,768]{2,1,0:T(8,128)(2,1)} %proj_in.1, bf16[2,224,256]{2,1,0:T(8,128)(2,1)} %bitcast.11, ...), custom_call_target="tpu_custom_call" | custom-call | tf_op jit(solution)/shard_map/two_blocks/pallas_call | solution.py:687
  236.8 0.0 copy-start
  236.8 3.0 %copy.15 = bf16[16,16,3584]{2,1,0:T(8,128)(2,1)} copy(bf16[16,16,3584]{2,1,0:T(8,128)(2,1)} %bitcast.7) | data formatting | bytes 3670016
  239.8 0.0 copy-done
  239.8 0.0 copy-start.1
  239.8 0.0 copy-start.2
  239.8 1.2 copy.16
  241.1 0.3 copy-done.1
  241.4 0.8 copy.17
  242.3 0.0 copy-done.2
  242.3 0.7 copy.18
Async XLA Ops:
  236.8 3.0 %copy-start = (bf16[256,3584]{1,0:T(8,128)(2,1)S(1)}, bf16[256,3584]{1,0:T(8,128)(2,1)}, u32[]{:S(2)}) copy-start(bf16[256,3584]{1,0:T(8,128)(2,1)} %get-tuple-element.9) | copy-start | bytes 5505028
  239.8 1.6 copy-start.1
  239.8 2.4 copy-start.2

commit v2 on v1

--- a/solution.py
+++ b/solution.py
@@ -96,13 +96,16 @@
         proj_ref[...] += product
 
 
-def branch(proj_ref, qkg, w_ref, att_ref, part_ref, temporal):
+def attend(proj_ref, qkg, att_ref, temporal):
     for head in range(2):
         parts = head_forward(proj_ref, qkg, head, temporal)
         att_ref[:, head * HD : (head + 1) * HD] = dot(parts[7].astype(BF16), parts[6]).astype(BF16)
+
+
+def branch(att_ref, w_ref, part_ref, cols):
     att = att_ref[...]
 
-    @pl.loop(0, NT)
+    @pl.loop(cols[0] // TILE, sum(cols) // TILE)
     def _(i):
         at = tile_at(i)
         part_ref[:, at] = dot(att, w_ref[at, PC:], ((1,), (1,))).astype(BF16)
@@ -112,7 +115,7 @@
     return (dy_ref[:, at].astype(F32) * gate[:, at]).astype(BF16)
 
 
-def backward(dy_ref, w_ref, gate, qkg, proj_ref, dpart_ref, datt_ref, dproj_ref, temporal):
+def attended_grad(dy_ref, w_ref, gate, datt_ref):
     datt_ref[...] = jnp.zeros_like(datt_ref)
 
     @pl.loop(0, NT)
@@ -120,25 +123,38 @@
         at = tile_at(i)
         datt_ref[...] += dot(scaled_tile(dy_ref, gate, at), w_ref[at, PC:])
 
+
+def projected_grad(qkg, proj_ref, datt_ref, dproj_ref, temporal):
     for head in range(2):
         d_att = datt_ref[:, head * HD : (head + 1) * HD].astype(BF16)
         head_backward(proj_ref, qkg, head, temporal, d_att, dproj_ref)
+
+
+def normed_grad(dproj_ref, w_ref, dpart_ref, cols):
     dproj = dproj_ref[...]
+
+    @pl.loop(cols[0] // TILE, sum(cols) // TILE)
+    def _(i):
+        at = tile_at(i)
+        dpart_ref[:, at] = dot(dproj, w_ref[at, :PC], ((1,), (1,))).astype(BF16)
+
+
+def proj_grads(normed_ref, dproj_ref, g_ref, cols):
+    to = pl.ds(*cols)
+    dproj = dproj_ref[:, to]
 
     @pl.loop(0, NT)
     def _(i):
         at = tile_at(i)
-        dpart_ref[:, at] = dot(dproj, w_ref[at, :PC], ((1,), (1,))).astype(BF16)
-
-
-def weight_grads(dy_ref, gate, normed_ref, att_ref, dproj_ref, g_ref):
-    dproj = dproj_ref[...]
+        g_ref[at, to] = dot(normed_ref[:, at], dproj, ((0,), (0,))).astype(BF16)
+
+
+def outw_grads(dy_ref, gate, att_ref, g_ref):
     att = att_ref[...]
 
     @pl.loop(0, NT)
     def _(i):
         at = tile_at(i)
-        g_ref[at, :PC] = dot(normed_ref[:, at], dproj, ((0,), (0,))).astype(BF16)
         g_ref[at, PC:] = dot(scaled_tile(dy_ref, gate, at), att, ((0,), (0,))).astype(BF16)
 
 
@@ -169,28 +185,30 @@
     return (s, 2 * lax.rem(f // 2 + dp + 4, 4) + lax.rem(f + dq, 2))
 
 
+def pair_of(device, sign):
+    s, f = device
+    x = lax.rem(s // 4 + sign * (f // 2) + 4, 4)
+    return 2 * x + lax.rem(s // 2 + f + f // 2, 2)
+
+
 def by_frames(dp, dq):
     device = fsdp_node(dp, dq)
-    return device, device[1] * OWN
+    return device, pair_of(device, -1) * OWN
 
 
 def by_positions(dp, dq):
-    s, _ = place()
     device = fsdp_node(dp, dq)
-    shifted = 2 * lax.rem(device[1] // 2 + s // 4, 4) + lax.rem(device[1], 2)
-    return device, shifted * OWN
+    return device, pair_of(device, 1) * OWN
 
 
 def swap_out():
-    s, _ = place()
-    pair = by_positions(0, 0)[1] // OWN
-    return [(2 * pair + e, s // 2) for e in range(2)]
+    s, f = place()
+    return [(2 * pair_of((s, f), 1) + e, f) for e in range(2)]
 
 
 def swap_back():
     s, f = place()
-    there = 2 * lax.rem(s // 4 - f // 2 + 4, 4) + lax.rem(s // 2, 2)
-    return [(2 * f + i, there) for i in range(2)]
+    return [(2 * pair_of((s, f), -1) + i, f) for i in range(2)]
 
 
 def is_me(device):
@@ -222,7 +240,7 @@
 
 
 class Gather:
-    MESSAGES = (
+    NEAR = (
         ((0, 0), None, (1, 0)),
         ((0, 0), None, (-1, 0)),
         ((0, 0), None, (0, 1)),
@@ -230,20 +248,21 @@
         ((1, 0), 1, (-1, 0)),
         ((0, 1), None, (1, 0)),
         ((0, 1), None, (-1, 0)),
-        ((2, 0), 0, (0, 1)),
-        ((2, 0), 1, (0, 1)),
     )
-
-    def __init__(self, ref, node, size, sems):
-        self.ref, self.node, self.size, self.sems = ref, node, size, sems
+    WIDE = (((2, 0), 0, (0, 1)), ((2, 0), 1, (0, 1)))
+    SLIM = (((-1, 1), 0, (1, 0)), ((1, 1), 1, (-1, 0)))
+
+    def __init__(self, ref, node, size, cols, sems, wide=True):
+        self.ref, self.node, self.size, self.cols, self.sems, self.wide = ref, node, size, cols, sems, wide
+        self.messages = self.NEAR + (self.WIDE if wide else self.SLIM)
 
     def copy(self, m):
-        shard, half, target = self.MESSAGES[m]
+        shard, half, target = self.messages[m]
         start, n = self.node(*shard)[1], self.size
         if half is not None:
             n = n // 2
             start = start + half * n
-        rows = self.ref.at[rows_at(start, n)]
+        rows = self.ref.at[rows_at(start, n), pl.ds(*self.cols)]
         return remote(rows, rows, self.sems.at[0, m], self.sems.at[1, m], self.node(*target)[0])
 
     def send(self, *messages):
@@ -254,26 +273,52 @@
         for m in messages:
             self.copy(m).wait_recv()
 
+    def pass_on(self, *shards):
+        pass
+
     def start(self):
         self.send(0, 1, 2)
+        self.pass_on(0)
 
     def middle(self):
         self.got(0)
         self.send(3)
+        self.pass_on(1)
         self.got(1)
         self.send(4)
+        self.pass_on(2)
         self.got(2)
         self.send(5, 6)
+        self.pass_on(3)
 
     def last(self):
-        self.got(3)
-        self.send(7)
-        self.got(4)
-        self.send(8)
+        if self.wide:
+            self.got(3)
+            self.send(7)
+            self.got(4)
+            self.send(8)
+            self.pass_on(4)
+        else:
+            self.got(5)
+            self.send(7)
+            self.pass_on(5)
+            self.got(6)
+            self.send(8)
+            self.pass_on(6)
+
+    def fifth(self):
+        if self.wide:
+            self.got(5)
+            self.pass_on(5)
+            self.got(6)
+            self.pass_on(6)
+        else:
+            self.got(3, 4)
+            self.pass_on(4)
 
     def end(self):
-        self.got(5, 6, 7, 8)
-        self.sent()
+        self.got(7, 8)
+        self.pass_on(7)
 
     def sent(self):
         for m in range(9):
@@ -283,22 +328,25 @@
 class Weights(Gather):
     SHARDS = ((0, 0), (-1, 0), (1, 0), (0, 1), (2, 0), (-1, 1), (1, 1), (2, 1))
 
-    def __init__(self, block, proj_ref, outw_ref, w_ref, sems, near_sems, local):
-        super().__init__(w_ref, seq_node, SH, sems)
+    def __init__(self, parts, w_ref, cols, sems, near_sems, local, wide):
+        super().__init__(w_ref, seq_node, SH, cols, sems, wide)
         self.near_sems = near_sems
         rows = rows_at(seq_node(0, 0)[1], SH)
         self.own = [
-            pltpu.make_async_copy(proj_ref.at[block], w_ref.at[rows, pl.ds(0, PC)], local.at[0]),
-            pltpu.make_async_copy(outw_ref.at[block], w_ref.at[rows, pl.ds(PC, WC - PC)], local.at[1]),
+            pltpu.make_async_copy(src, w_ref.at[rows, pl.ds(*at)], local.at[i]) for i, (src, at) in enumerate(parts)
         ]
 
     def near(self, n):
-        rows = self.ref.at[rows_at(self.node(*self.SHARDS[n])[1], SH)]
+        rows = self.ref.at[rows_at(self.node(*self.SHARDS[n])[1], SH), pl.ds(*self.cols)]
         return remote(rows, rows, self.near_sems.at[0, n], self.near_sems.at[1, n], sibling())
 
     def near_got(self, *shards):
         for n in shards:
             self.near(n).wait_recv()
+
+    def pass_on(self, *shards):
+        for n in shards:
+            self.near(n).start()
 
     def load(self):
         for copy in self.own:
@@ -308,32 +356,6 @@
         for copy in self.own:
             copy.wait()
         super().start()
-        self.near(0).start()
-
-    def middle(self):
-        self.got(0)
-        self.send(3)
-        self.near(1).start()
-        self.got(1)
-        self.send(4)
-        self.near(2).start()
-        self.got(2)
-        self.send(5, 6)
-        self.near(3).start()
-
-    def last(self):
-        super().last()
-        self.near(4).start()
-
-    def fifth(self):
-        self.got(5)
-        self.near(5).start()
-        self.got(6)
-        self.near(6).start()
-
-    def end(self):
-        self.got(7, 8)
-        self.near(7).start()
 
     def sent(self):
         super().sent()
@@ -341,15 +363,17 @@
             self.near(n).wait_send()
 
 
-def add_rows(ref, start, n, stage):
+def add_rows(ref, start, n, cols, stage, base):
+    at = pl.ds(*cols)
+
     @pl.loop(0, n // 16)
     def _(i):
-        rows, here = rows_at(start + i * 16, 16), rows_at(i * 16, 16)
-        ref[rows, :] = (ref[rows, :].astype(F32) + stage[here, :].astype(F32)).astype(BF16)
+        rows, here = rows_at(start + i * 16, 16), rows_at(base + i * 16, 16)
+        ref[rows, at] = (ref[rows, at].astype(F32) + stage[here, at].astype(F32)).astype(BF16)
 
 
 class Reduce:
-    MESSAGES = (
+    NEAR = (
         ((-1, 0), None, (-1, 0), 5),
         ((1, 0), None, (1, 0), 6),
         ((0, 1), None, (0, 1), 4),
@@ -357,20 +381,23 @@
         ((2, 0), 1, (1, 0), 3),
         ((-1, 1), None, (-1, 0), 1),
         ((1, 1), None, (1, 0), 2),
-        ((2, 1), None, (0, 1), 0),
     )
-
-    def __init__(self, ref, node, size, held, sems):
-        self.ref, self.node, self.size, self.held, self.sems = ref, node, size, held, sems
+    WIDE = (((2, 1), None, (0, 1), 0),)
+    SLIM = (((2, 1), 0, (-1, 0), 0), ((2, 1), 1, (1, 0), 0))
+
+    def __init__(self, ref, node, size, cols, held, sems, wide=True):
+        self.ref, self.node, self.size, self.cols, self.held, self.sems = ref, node, size, cols, held, sems
+        self.wide = wide
+        self.messages = self.NEAR + (self.WIDE if wide else self.SLIM)
 
     def copy(self, m):
-        shard, half, target, slot = self.MESSAGES[m]
+        shard, half, target, slot = self.messages[m]
         start, n, first = self.node(*shard)[1], self.size, 0
         if half is not None:
             n = n // 2
             first = half * n
-        src = self.ref.at[rows_at(start + first, n)]
-        dst = self.held.at[pl.ds(slot * self.size + first, n)]
+        src = self.ref.at[rows_at(start + first, n), pl.ds(*self.cols)]
+        dst = self.held.at[pl.ds(slot * self.size + first, n), pl.ds(*self.cols)]
         return remote(src, dst, self.sems.at[0, m], self.sems.at[1, m], self.node(*target)[0])
 
     def send(self, *messages):
@@ -386,41 +413,69 @@
         if half is not None:
             n = n // 2
             first = half * n
-        add_rows(self.ref, start + first, n, self.held.at[pl.ds(slot * self.size + first, n)])
+        add_rows(self.ref, start + first, n, self.cols, self.held, slot * self.size + first)
 
     def ready(self, *shards):
         pass
 
     def start(self):
-        self.ready(0, 1, 2)
-        self.send(7, 5, 6)
+        if self.wide:
+            self.ready((2, 1), (-1, 1), (1, 1))
+            self.send(7, 5, 6)
+        else:
+            self.ready((2, 1))
+            self.send(7, 8)
+            self.ready((2, 0))
+            self.send(3, 4)
 
     def middle(self):
-        self.ready(3)
-        self.got(7)
-        self.add((2, 0), 0)
-        self.send(3, 4)
-        self.ready(4)
-        self.got(5)
-        self.add((0, 1), 1)
-        self.got(6)
-        self.add((0, 1), 2)
-        self.send(2)
-
-    def last(self):
-        self.ready(5)
+        if self.wide:
+            self.ready((2, 0))
+            self.got(7)
+            self.add((2, 0), 0)
+            self.send(3, 4)
+            self.ready((0, 1))
+            self.got(5)
+            self.add((0, 1), 1)
+            self.got(6)
+            self.add((0, 1), 2)
+            self.send(2)
+        else:
+            self.ready((-1, 1))
+            self.got(7)
+            self.add((-1, 1), 0, 0)
+            self.send(5)
+            self.ready((1, 1))
+            self.got(8)
+            self.add((1, 1), 0, 1)
+            self.send(6)
+            self.nearest()
+
+    def nearest(self):
+        self.ready((-1, 0))
         self.got(3)
         self.add((-1, 0), 3, 0)
         self.send(0)
-        self.ready(6)
+        self.ready((1, 0))
         self.got(4)
         self.add((1, 0), 3, 1)
         self.send(1)
 
+    def last(self):
+        if self.wide:
+            self.nearest()
+        else:
+            self.ready((0, 1))
+            self.got(5)
+            self.add((0, 1), 1)
+            self.got(6)
+            self.add((0, 1), 2)
+            self.send(2)
+
     def end(self):
-        self.ready(7)
+        self.ready((0, 0))
         self.got(0, 1, 2)
-        for m in range(8):
+        for m in range(len(self.messages)):
             self.copy(m).wait_send()
 
     def total(self, at):
@@ -431,24 +486,26 @@
 
 
 class WeightGrads(Reduce):
-    SHARDS = ((2, 1), (-1, 1), (1, 1), (2, 0), (0, 1), (-1, 0), (1, 0), (0, 0))
-
-    def __init__(self, ref, held, sems, near_held, near_sems):
-        super().__init__(ref, seq_node, SH, held, sems)
+    SHARDS = ((2, 1), (2, 0), (-1, 1), (1, 1), (-1, 0), (1, 0), (0, 1), (0, 0))
+
+    def __init__(self, ref, cols, held, sems, near_held, near_sems):
+        super().__init__(ref, seq_node, SH, cols, held, sems, False)
         self.near_held, self.near_sems = near_held, near_sems
 
     def near(self, n):
         s, _ = place()
         start = self.node(*self.SHARDS[n])[1] + (1 - 2 * lax.rem(s, 2)) * SH
         return remote(
-            self.ref.at[rows_at(start, SH)], self.near_held.at[pl.ds(n * SH, SH)],
+            self.ref.at[rows_at(start, SH), pl.ds(*self.cols)],
+            self.near_held.at[pl.ds(n * SH, SH), pl.ds(*self.cols)],
             self.near_sems.at[0, n], self.near_sems.at[1, n], sibling(),
         )
 
     def ready(self, *shards):
-        for n in shards:
+        for shard in shards:
+            n = self.SHARDS.index(shard)
             self.near(n).wait_recv()
-            add_rows(self.ref, self.node(*self.SHARDS[n])[1], SH, self.near_held.at[pl.ds(n * SH, SH)])
+            add_rows(self.ref, self.node(*shard)[1], SH, self.cols, self.near_held, n * SH)
 
     def pair(self):
         for n in range(8):
@@ -456,31 +513,46 @@
 
     def result(self, block, gproj_ref, goutw_ref):
         base = self.node(0, 0)[1]
+        at = pl.ds(*self.cols)
 
         @pl.loop(0, SH // 16)
         def _(i):
             rows, here = rows_at(base + i * 16, 16), rows_at(i * 16, 16)
-            total = self.ref[rows, :].astype(F32)
+            total = self.ref[rows, at].astype(F32)
             for slot in (4, 5, 6):
-                total = total + self.held[rows_at(slot * SH + i * 16, 16), :].astype(F32)
-            gproj_ref[block, here, :] = total[:, :PC].astype(BF16)
-            goutw_ref[block, here, :] = total[:, PC:].astype(BF16)
+                total = total + self.held[rows_at(slot * SH + i * 16, 16), at].astype(F32)
+            if self.cols[0] < PC:
+                gproj_ref[block, here, at] = total.astype(BF16)
+            else:
+                goutw_ref[block, here, :] = total.astype(BF16)
 
         for n in range(8):
             self.near(n).wait_send()
 
 
+class Parts:
+    def __init__(self, *parts):
+        self.parts = parts
+
+    def __getattr__(self, step):
+        def run(*args):
+            for part in self.parts:
+                getattr(part, step)(*args)
+
+        return run
+
+
 class Swap:
-    def __init__(self, src_ref, dst_ref, targets, sources, base, sems, local):
+    def __init__(self, src_ref, dst_ref, cols, targets, base, sems, local):
         self.src_ref, self.dst_ref, self.targets, self.base = src_ref, dst_ref, targets, base
-        self.sources, self.sems, self.local = sources, sems, local
+        self.cols, self.sems, self.local = pl.ds(*cols), sems, local
 
     def each(self, act):
         s, _ = place()
         for j in range(2):
-            src = self.src_ref.at[pl.ds(j * 16, 16)]
-            there = self.dst_ref.at[rows_at(s * 16, 16)]
-            here = self.dst_ref.at[rows_at(self.base + j * 16, 16)]
+            src = self.src_ref.at[pl.ds(j * 16, 16), self.cols]
+            there = self.dst_ref.at[rows_at(s * 16, 16), self.cols]
+            here = self.dst_ref.at[rows_at(self.base + j * 16, 16), self.cols]
             act(j, src, there, here)
 
     def start(self):
@@ -516,8 +588,8 @@
         self.each(act)
 
 
-def branch_end(x_ref, x_base, gate, reduced, out_ref):
-    @pl.loop(0, NT)
+def branch_end(x_ref, x_base, gate, reduced, out_ref, cols):
+    @pl.loop(cols[0] // TILE, sum(cols) // TILE)
     def _(i):
         at = tile_at(i)
         value = x_ref[rows_at(x_base, OWN), at].astype(F32) + gate[:, at] * reduced.total(at)
@@ -557,119 +629,219 @@
     x_group = s // 4
     gain0, gain1, gate0, gate1 = (r.at[pl.ds(b, 1)] for r in (gain_ref, gate_ref) for b in range(2))
     qkg0, qkg1 = qkg_ref[0], qkg_ref[1]
-    w0 = Weights(0, proj_in, outw_in, w0_ref, w_sems.at[0], wn_sems.at[0], local.at[0])
-    w1 = Weights(1, proj_in, outw_in, w1_ref, w_sems.at[1], wn_sems.at[1], local.at[1])
+    proj_cols, outw_cols = (0, PC), (PC, WC - PC)
+    w0p = Weights(
+        [(proj_in.at[0], proj_cols)], w0_ref, proj_cols, w_sems.at[0], wn_sems.at[0], local.at[0], True
+    )
+    w0o = Weights(
+        [(outw_in.at[0], outw_cols)], w0_ref, outw_cols, w_sems.at[1], wn_sems.at[1], local.at[1], True
+    )
+    w1 = [
+        Weights([(src, cols)], w1_ref, cols, w_sems.at[2 + i], wn_sems.at[2 + i], local.at[2 + i], False)
+        for i, (src, cols) in enumerate(
+            (
+                (proj_in.at[1, :, pl.ds(0, 384)], (0, 384)),
+                (proj_in.at[1, :, pl.ds(384, 384)], (384, 384)),
+                (outw_in.at[1], outw_cols),
+            )
+        )
+    ]
     positions, frames = by_positions(0, 0)[1], by_frames(0, 0)[1]
-
-    w0.load()
-    w1.load()
+    whole_rows, halves = (0, D), ((0, 2048), (2048, 1536))
+    shards = range(8)
+
+    def two(make, *args):
+        return Parts(*(make(cols, i, *args) for i, cols in enumerate(halves)))
+
+    def reduce_of(cols, i, node, held, first_sem):
+        return Reduce(part_ref, node, OWN, cols, held_ref.at[held], rs_sems.at[first_sem + i])
+
+    def gather_of(cols, i, ref, node, first_sem):
+        return Gather(ref, node, OWN, cols, ag_sems.at[first_sem + i])
+
+    w0p.load()
+    w0o.load()
+    for weights in w1:
+        weights.load()
     greet()
-    w0.start()
+    w0p.start()
     normalise(x_ref, gain0, normed0_ref)
-    w0.middle()
-    w0.near_got(0, 3)
+    w0o.start()
+    w0p.middle()
+    w0o.middle()
+    w0p.near_got(0, 3)
     project(x_group, normed0_ref, w0_ref, proj0_ref, True)
-    w0.last()
-    w0.fifth()
-    w1.start()
-    w0.near_got(1, 5)
+    w0p.last()
+    w0p.fifth()
+    w0p.near_got(1, 5)
     project(lax.rem(x_group + 3, 4), normed0_ref, w0_ref, proj0_ref, False)
-    w0.near_got(2, 6)
+    w0p.near_got(2, 6)
     project(lax.rem(x_group + 1, 4), normed0_ref, w0_ref, proj0_ref, False)
-    w0.end()
-    w0.near_got(4, 7)
+    w0o.last()
+    w0p.end()
+    w0p.near_got(4, 7)
+    w1[0].start()
     project(lax.rem(x_group + 2, 4), normed0_ref, w0_ref, proj0_ref, False)
-    branch(proj0_ref, qkg0, w0_ref, att0_ref, part_ref, False)
-
-    r0 = Reduce(part_ref, by_positions, OWN, held_ref.at[0], rs_sems.at[0])
-    r0.start()
-    w1.middle()
+    attend(proj0_ref, qkg0, att0_ref, False)
+    w0o.fifth()
+    w0o.end()
+    w0o.near_got(*shards)
+
+    r0 = two(reduce_of, by_positions, 0, 0)
+    for piece, cols in zip(r0.parts, halves):
+        branch(att0_ref, w0_ref, part_ref, cols)
+        piece.start()
+    w1[0].middle()
+    w1[1].start()
     r0.middle()
+    w1[0].last()
     r0.last()
-    w1.last()
-    r0.end()
-    branch_end(x_ref, positions, gate0, r0, own_ref.at[0])
-    out = Swap(own_ref.at[0], middle_ref, swap_out(), None, frames, swap_sems.at[0], local.at[2, 0])
-    out.start()
-    w1.fifth()
-    out.wait()
-    a0 = Gather(middle_ref, by_frames, OWN, ag_sems.at[0])
-    a0.start()
-    w1.end()
+    swaps = []
+    for i, cols in enumerate(halves):
+        r0.parts[i].end()
+        branch_end(x_ref, positions, gate0, r0.parts[i], own_ref.at[0], cols)
+        swaps.append(
+            Swap(own_ref.at[0], middle_ref, cols, swap_out(), frames, swap_sems.at[i], local.at[5, i])
+        )
+        swaps[i].start()
+        if i == 0:
+            w1[1].middle()
+    a0 = two(gather_of, middle_ref, by_frames, 0)
+    for i in range(2):
+        swaps[i].wait()
+        a0.parts[i].start()
+    w1[1].last()
+    w1[2].start()
+    w1[0].fifth()
+    w1[0].end()
     a0.middle()
+    w1[2].middle()
+    w1[1].fifth()
+    w1[1].end()
     a0.last()
-    w0.sent()
-    w1.sent()
-    w1.near_got(0, 1, 2, 3, 4, 5, 6, 7)
+    w1[2].last()
+    w1[2].fifth()
+    w1[2].end()
+    for weights in (w0p, w0o, *w1):
+        weights.sent()
+    for weights in w1:
+        weights.near_got(*shards)
+    attended_grad(dy_ref, w1_ref, gate1, datt_ref)
+    a0.fifth()
     a0.end()
+    a0.sent()
 
     normalise(middle_ref, gain1, normed1_ref)
     for group in range(4):
         project(group, normed1_ref, w1_ref, proj1_ref, group == 0)
-    branch(proj1_ref, qkg1, w1_ref, att1_ref, part1_ref, True)
-    r1 = Reduce(part1_ref, by_frames, OWN, held_ref.at[1], rs_sems.at[1])
+    attend(proj1_ref, qkg1, att1_ref, True)
+    branch(att1_ref, w1_ref, part1_ref, whole_rows)
+    r1 = Reduce(part1_ref, by_frames, OWN, whole_rows, held_ref.at[1], rs_sems.at[2])
     r1.start()
-    backward(dy_ref, w1_ref, gate1, qkg1, proj1_ref, part_ref, datt_ref, dproj_ref, True)
-
-    r2 = Reduce(part_ref, by_frames, OWN, held_ref.at[2], rs_sems.at[2])
-    r2.start()
+    grad_cols = ((PC, WC - PC), (0, 384), (384, 384))
+    grads1 = [
+        WeightGrads(g_ref, cols, far1_ref, g_sems.at[i], near1_ref, gn_sems.at[i]) for i, cols in enumerate(grad_cols)
+    ]
+    outw_grads(dy_ref, gate1, att1_ref, g_ref)
+    grads1[0].pair()
+    projected_grad(qkg1, proj1_ref, datt_ref, dproj_ref, True)
+
+    r2 = two(reduce_of, by_frames, 2, 3)
+    for piece, cols in zip(r2.parts, halves):
+        normed_grad(dproj_ref, w1_ref, part_ref, cols)
+        piece.start()
+    grads1[0].start()
+    for i in (1, 2):
+        proj_grads(normed1_ref, dproj_ref, g_ref, grad_cols[i])
+        grads1[i].pair()
+    r2.middle()
+    grads1[1].start()
     r1.middle()
-    weight_grads(dy_ref, gate1, normed1_ref, att1_ref, dproj_ref, g_ref)
-    grads1 = WeightGrads(g_ref, far1_ref, g_sems.at[1], near1_ref, gn_sems.at[1])
-    grads1.pair()
-    r2.middle()
+    r2.last()
+    grads1[0].middle()
+    r2.end()
+    input_grad(middle_ref, frames, dy_ref, frames, gain1, r2.parts[0], sum_ref, own_ref.at[1])
+    a1 = two(gather_of, grad_ref, by_positions, 2)
+    swaps = [
+        Swap(own_ref.at[1], grad_ref, cols, swap_back(), positions, swap_sems.at[2 + i], local.at[5, i])
+        for i, cols in enumerate(halves)
+    ]
+    for i in range(2):
+        swaps[i].start()
     r1.last()
-    r2.last()
-    grads1.start()
-    r2.end()
-    input_grad(middle_ref, frames, dy_ref, frames, gain1, r2, sum_ref, own_ref.at[1])
-    back = Swap(own_ref.at[1], grad_ref, swap_back(), None, positions, swap_sems.at[1], local.at[2, 0])
-    back.start()
+    grads1[0].last()
+    for i in range(2):
+        swaps[i].wait()
+        a1.parts[i].start()
+    grads1[1].middle()
+    a1.middle()
+    grads1[2].start()
+    a1.last()
+    grads1[1].last()
     r1.end()
-    branch_end(middle_ref, frames, gate1, r1, own_ref.at[2])
-    keep = pltpu.make_async_copy(own_ref.at[2], mixed_ref.at[rows_at(frames, OWN)], local.at[2, 1])
-    keep.start()
-    back.wait()
-    a1 = Gather(grad_ref, by_positions, OWN, ag_sems.at[1])
-    a1.start()
-    grads1.middle()
-    a1.middle()
-    grads1.last()
-    a1.last()
-    keep.wait()
-    a2 = Gather(mixed_ref, by_frames, OWN, ag_sems.at[2])
-    a2.start()
-    grads1.end()
-    grads1.result(1, gproj_ref, goutw_ref)
-    a1.end()
-
-    backward(grad_ref, w0_ref, gate0, qkg0, proj0_ref, part_ref, datt_ref, dproj_ref, False)
-    r3 = Reduce(part_ref, by_positions, OWN, held_ref.at[3], rs_sems.at[3])
-    r3.start()
-    a2.middle()
-    weight_grads(grad_ref, gate0, normed0_ref, att0_ref, dproj_ref, g_ref)
-    near0_ref, far0_ref = w1_ref.at[pl.ds(0, 8 * SH)], w1_ref.at[pl.ds(8 * SH, 7 * SH)]
-    grads0 = WeightGrads(g_ref, far0_ref, g_sems.at[0], near0_ref, gn_sems.at[0])
-    grads0.pair()
-    r3.middle()
-    r3.last()
-    grads0.start()
-    a2.last()
-    r3.end()
-    input_grad(x_ref, positions, grad_ref, positions, gain0, r3, sum_ref, own_ref.at[3])
-    keep = pltpu.make_async_copy(own_ref.at[3], clip_ref.at[rows_at(positions, OWN)], local.at[2, 1])
+    branch_end(middle_ref, frames, gate1, r1, own_ref.at[2], whole_rows)
+    keep = pltpu.make_async_copy(own_ref.at[2], mixed_ref.at[rows_at(frames, OWN)], local.at[6, 0])
     keep.start()
     keep.wait()
-    a3 = Gather(clip_ref, by_positions, OWN, ag_sems.at[3])
+    a1.fifth()
+    a2 = Gather(mixed_ref, by_frames, OWN, whole_rows, ag_sems.at[4])
+    a2.start()
+    grads1[2].middle()
+    a1.end()
+
+    attended_grad(grad_ref, w0_ref, gate0, datt_ref)
+    projected_grad(qkg0, proj0_ref, datt_ref, dproj_ref, False)
+    r3 = two(reduce_of, by_positions, 3, 5)
+    for piece, cols in zip(r3.parts, halves):
+        normed_grad(dproj_ref, w0_ref, part_ref, cols)
+        piece.start()
+    near0_ref, far0_ref = w1_ref.at[pl.ds(0, 8 * SH)], w1_ref.at[pl.ds(8 * SH, 7 * SH)]
+    grads0 = [
+        WeightGrads(w0_ref, cols, far0_ref, g_sems.at[3 + i], near0_ref, gn_sems.at[3 + i])
+        for i, cols in enumerate(grad_cols)
+    ]
+    proj_grads(normed0_ref, dproj_ref, w0_ref, grad_cols[1])
+    grads0[1].pair()
+    a2.middle()
+    proj_grads(normed0_ref, dproj_ref, w0_ref, grad_cols[2])
+    grads0[2].pair()
+    r3.middle()
+    grads0[1].start()
+    outw_grads(grad_ref, gate0, att0_ref, w0_ref)
+    grads0[0].pair()
+    r3.last()
+    grads0[2].start()
+    grads1[2].last()
+    grads0[1].middle()
+    r3.end()
+    input_grad(x_ref, positions, grad_ref, positions, gain0, r3.parts[0], sum_ref, own_ref.at[3])
+    keep = pltpu.make_async_copy(own_ref.at[3], clip_ref.at[rows_at(positions, OWN)], local.at[6, 1])
+    keep.start()
+    grads0[0].start()
+    keep.wait()
+    a3 = two(gather_of, clip_ref, by_positions, 5)
     a3.start()
-    grads0.middle()
+    a2.last()
+    grads0[2].middle()
+    grads0[0].middle()
     a3.middle()
-    grads0.last()
+    grads0[1].last()
     a3.last()
+    grads0[2].last()
+    for i in range(3):
+        grads1[i].end()
+        grads1[i].result(1, gproj_ref, goutw_ref)
+    grads0[0].last()
+    a1.sent()
+    a2.fifth()
     a2.end()
-    grads0.end()
-    grads0.result(0, gproj_ref, goutw_ref)
+    a2.sent()
+    a3.fifth()
+    for i in (1, 2, 0):
+        grads0[i].end()
+        grads0[i].result(0, gproj_ref, goutw_ref)
     a3.end()
+    a3.sent()
 
 
 def shaped(shape, dtype=BF16):
@@ -710,14 +882,14 @@
             pltpu.VMEM((OWN, D), F32),
             pltpu.VMEM((8 * SH, WC), BF16),
             pltpu.VMEM((7 * SH, WC), BF16),
-            sem(2, 2, 9),
-            sem(2, 2, 8),
-            sem(3, 2),
-            sem(4, 2, 8),
-            sem(4, 2, 9),
-            sem(2, 2, 8),
-            sem(2, 2, 8),
-            sem(2, 2, 2),
+            sem(5, 2, 9),
+            sem(5, 2, 8),
+            sem(7, 2),
+            sem(7, 2, 9),
+            sem(7, 2, 9),
+            sem(6, 2, 9),
+            sem(6, 2, 8),
+            sem(4, 2, 2),
         ],
         compiler_params=pltpu.CompilerParams(
             vmem_limit_bytes=VMEM_LIMIT, collective_id=0, has_side_effects=True

time: 243 us -> 209 us (0.86)
  Pallas kernels: 236 us -> 201 us
    pallas_call x1, Pallas kernels: 236 us -> 201 us  [local_program(): pl.pallas_call(whole, out_shape=[shaped((T, D)), shaped((T, D)), shaped((...]
where the time goes in v2:
time: 209 us; the launch traced here: 208 us
  Pallas kernels  201 us (96%)
  local copies, waits for them, and re-layouts  6.09 us (3%)
    pallas_call x1, Pallas kernels, local_program(): pl.pallas_call(whole, out_shape=[shaped((T, D)), shaped((T, D)), shaped((...  201 us
    unnamed x10, local copies, waits for them, and re-layouts  6.09 us

profile of v2, /device:TPU:8, one launch (start us, length us, event | category | flops | bytes accessed | tf_op | source)
XLA Modules:
  0.0 207.9 jit_solution(9587697956620613573)
XLA Ops:
  0.6 201.2 %two_blocks.1 = (bf16[256,3584]{1,0:T(8,128)(2,1)}, bf16[256,3584]{1,0:T(8,128)(2,1)}, bf16[2,224,768]{2,1,0:T(8,128)(2,1)}, bf16[2,224,256]{2,1,0:T(8,128)(2,1)}) custom-call(bf16[256,3584]{1,0:T(8,128)(2,1)} %bitcast.8, bf16[256,3584]{1,0:T(8,128)(2,1)} %bitcast.9, bf16[2,224,768]{2,1,0:T(8,128)(2,1)} %proj_in.1, bf16[2,224,256]{2,1,0:T(8,128)(2,1)} %bitcast.11, ...), custom_call_target="tpu_custom_call" | custom-call | tf_op jit(solution)/shard_map/two_blocks/pallas_call | solution.py:859
  201.8 0.0 copy-start
  201.8 3.0 %copy.15 = bf16[16,16,3584]{2,1,0:T(8,128)(2,1)} copy(bf16[16,16,3584]{2,1,0:T(8,128)(2,1)} %bitcast.7) | data formatting | bytes 3670016
  204.8 0.0 copy-done
  204.8 0.0 copy-start.1
  204.8 0.0 copy-start.2
  204.8 1.2 copy.16
  206.1 0.3 copy-done.1
  206.4 0.8 copy.17
  207.2 0.0 copy-done.2
  207.3 0.7 copy.18
Async XLA Ops:
  201.8 3.0 %copy-start = (bf16[256,3584]{1,0:T(8,128)(2,1)S(1)}, bf16[256,3584]{1,0:T(8,128)(2,1)}, u32[]{:S(2)}) copy-start(bf16[256,3584]{1,0:T(8,128)(2,1)} %get-tuple-element.9) | copy-start | bytes 5505028
  204.8 1.6 copy-start.1
  204.8 2.4 %copy-start.2 = (bf16[2,224,256]{2,1,0:T(8,128)(2,1)S(1)}, bf16[2,224,256]{2,1,0:T(8,128)(2,1)}, u32[]{:S(2)}) copy-start(bf16[2,224,256]{2,1,0:T(8,128)(2,1)} %get-tuple-element.11) | copy-start | bytes 688132

commit v3 on v2

--- a/solution.py
+++ b/solution.py
@@ -19,9 +19,10 @@
 PC = 768
 TILE = 512
 NT = D // TILE
+PART = 896
 F32 = jnp.float32
 BF16 = jnp.bfloat16
-VMEM_LIMIT = 60 * 1024 * 1024
+VMEM_LIMIT = 55 * 1024 * 1024
 
 
 def tile_at(i, size=TILE):
@@ -87,6 +88,16 @@
         normed_ref[:, at] = (x_ref[:, at].astype(F32) * inverse * gain[:, at]).astype(BF16)
 
 
+def project_scaled(x_ref, w_ref, gain, proj_ref, cols, squares):
+    def step(i, squares):
+        at = tile_at(i, PART)
+        x = x_ref[:, at].astype(F32)
+        proj_ref[...] += dot((x * gain[:, at]).astype(BF16), w_ref[at, :PC])
+        return squares + jnp.sum(x * x, -1, keepdims=True)
+
+    return lax.fori_loop(cols[0] // PART, sum(cols) // PART, step, squares)
+
+
 def project(group, normed_ref, w_ref, proj_ref, first):
     at = tile_at(group, GROUP)
     product = dot(normed_ref[:, at], w_ref[at, :PC])
@@ -105,9 +116,9 @@
 def branch(att_ref, w_ref, part_ref, cols):
     att = att_ref[...]
 
-    @pl.loop(cols[0] // TILE, sum(cols) // TILE)
+    @pl.loop(cols[0] // PART, sum(cols) // PART)
     def _(i):
-        at = tile_at(i)
+        at = tile_at(i, PART)
         part_ref[:, at] = dot(att, w_ref[at, PC:], ((1,), (1,))).astype(BF16)
 
 
@@ -115,12 +126,13 @@
     return (dy_ref[:, at].astype(F32) * gate[:, at]).astype(BF16)
 
 
-def attended_grad(dy_ref, w_ref, gate, datt_ref):
-    datt_ref[...] = jnp.zeros_like(datt_ref)
-
-    @pl.loop(0, NT)
+def attended_grad(dy_ref, w_ref, gate, datt_ref, cols):
+    if cols[0] == 0:
+        datt_ref[...] = jnp.zeros_like(datt_ref)
+
+    @pl.loop(cols[0] // PART, sum(cols) // PART)
     def _(i):
-        at = tile_at(i)
+        at = tile_at(i, PART)
         datt_ref[...] += dot(scaled_tile(dy_ref, gate, at), w_ref[at, PC:])
 
 
@@ -133,9 +145,9 @@
 def normed_grad(dproj_ref, w_ref, dpart_ref, cols):
     dproj = dproj_ref[...]
 
-    @pl.loop(cols[0] // TILE, sum(cols) // TILE)
+    @pl.loop(cols[0] // PART, sum(cols) // PART)
     def _(i):
-        at = tile_at(i)
+        at = tile_at(i, PART)
         dpart_ref[:, at] = dot(dproj, w_ref[at, :PC], ((1,), (1,))).astype(BF16)
 
 
@@ -149,12 +161,12 @@
         g_ref[at, to] = dot(normed_ref[:, at], dproj, ((0,), (0,))).astype(BF16)
 
 
-def outw_grads(dy_ref, gate, att_ref, g_ref):
+def outw_grads(dy_ref, gate, att_ref, g_ref, cols):
     att = att_ref[...]
 
-    @pl.loop(0, NT)
+    @pl.loop(cols[0] // PART, sum(cols) // PART)
     def _(i):
-        at = tile_at(i)
+        at = tile_at(i, PART)
         g_ref[at, PC:] = dot(scaled_tile(dy_ref, gate, at), att, ((0,), (0,))).astype(BF16)
 
 
@@ -588,15 +600,15 @@
         self.each(act)
 
 
-def branch_end(x_ref, x_base, gate, reduced, out_ref, cols):
-    @pl.loop(cols[0] // TILE, sum(cols) // TILE)
+def branch_end(x_ref, x_base, gate, reduced, out_ref, base, cols):
+    @pl.loop(cols[0] // PART, sum(cols) // PART)
     def _(i):
-        at = tile_at(i)
+        at = tile_at(i, PART)
         value = x_ref[rows_at(x_base, OWN), at].astype(F32) + gate[:, at] * reduced.total(at)
-        out_ref[:, at] = value.astype(BF16)
-
-
-def input_grad(x_ref, x_base, dy_ref, dy_base, gain, reduced, sum_ref, out_ref):
+        out_ref[rows_at(base, OWN), at] = value.astype(BF16)
+
+
+def input_grad(x_ref, x_base, dy_ref, dy_base, gain, reduced, sum_ref, out_ref, base):
     def moments(i, carry):
         squares, cross = carry
         at = tile_at(i)
@@ -615,13 +627,13 @@
         at = tile_at(i)
         x = x_ref[rows_at(x_base, OWN), at].astype(F32)
         value = dy_ref[rows_at(dy_base, OWN), at].astype(F32) + (inverse * sum_ref[:, at] - x * factor)
-        out_ref[:, at] = value.astype(BF16)
+        out_ref[rows_at(base, OWN), at] = value.astype(BF16)
 
 
 def whole(
-    x_ref, dy_ref, proj_in, outw_in, gain_ref, gate_ref, qkg_ref,
+    x_in, dy_in, proj_in, outw_in, gain_ref, gate_ref, qkg_ref,
     mixed_ref, clip_ref, gproj_ref, goutw_ref,
-    w0_ref, w1_ref, g_ref, normed0_ref, normed1_ref, proj0_ref, proj1_ref, att0_ref, att1_ref, datt_ref, dproj_ref,
+    x_ref, dy_ref, w0_ref, w1_ref, g_ref, normed0_ref, normed1_ref, proj0_ref, proj1_ref, att0_ref, att1_ref, datt_ref, dproj_ref,
     part_ref, part1_ref, middle_ref, grad_ref, held_ref, own_ref, sum_ref, near1_ref, far1_ref,
     w_sems, wn_sems, local, rs_sems, ag_sems, g_sems, gn_sems, swap_sems,
 ):
@@ -640,31 +652,36 @@
         Weights([(src, cols)], w1_ref, cols, w_sems.at[2 + i], wn_sems.at[2 + i], local.at[2 + i], False)
         for i, (src, cols) in enumerate(
             (
+                (outw_in.at[1], outw_cols),
                 (proj_in.at[1, :, pl.ds(0, 384)], (0, 384)),
                 (proj_in.at[1, :, pl.ds(384, 384)], (384, 384)),
-                (outw_in.at[1], outw_cols),
             )
         )
     ]
     positions, frames = by_positions(0, 0)[1], by_frames(0, 0)[1]
-    whole_rows, halves = (0, D), ((0, 2048), (2048, 1536))
+    whole_rows, halves = (0, D), [(0, 2 * PART), (2 * PART, 2 * PART)]
     shards = range(8)
 
-    def two(make, *args):
+    def parted(make, *args):
         return Parts(*(make(cols, i, *args) for i, cols in enumerate(halves)))
 
     def reduce_of(cols, i, node, held, first_sem):
         return Reduce(part_ref, node, OWN, cols, held_ref.at[held], rs_sems.at[first_sem + i])
 
-    def gather_of(cols, i, ref, node, first_sem):
-        return Gather(ref, node, OWN, cols, ag_sems.at[first_sem + i])
+    def gather_of(cols, i, ref, node, first_sem, wide=True):
+        return Gather(ref, node, OWN, cols, ag_sems.at[first_sem + i], wide)
 
     w0p.load()
     w0o.load()
     for weights in w1:
         weights.load()
+    x_load = pltpu.make_async_copy(x_in, x_ref, local.at[6, 0])
+    dy_load = pltpu.make_async_copy(dy_in, dy_ref, local.at[6, 1])
+    x_load.start()
+    dy_load.start()
     greet()
     w0p.start()
+    x_load.wait()
     normalise(x_ref, gain0, normed0_ref)
     w0o.start()
     w0p.middle()
@@ -673,11 +690,11 @@
     project(x_group, normed0_ref, w0_ref, proj0_ref, True)
     w0p.last()
     w0p.fifth()
+    w0o.last()
     w0p.near_got(1, 5)
     project(lax.rem(x_group + 3, 4), normed0_ref, w0_ref, proj0_ref, False)
     w0p.near_got(2, 6)
     project(lax.rem(x_group + 1, 4), normed0_ref, w0_ref, proj0_ref, False)
-    w0o.last()
     w0p.end()
     w0p.near_got(4, 7)
     w1[0].start()
@@ -687,7 +704,7 @@
     w0o.end()
     w0o.near_got(*shards)
 
-    r0 = two(reduce_of, by_positions, 0, 0)
+    r0 = parted(reduce_of, by_positions, 0, 0)
     for piece, cols in zip(r0.parts, halves):
         branch(att0_ref, w0_ref, part_ref, cols)
         piece.start()
@@ -699,14 +716,14 @@
     swaps = []
     for i, cols in enumerate(halves):
         r0.parts[i].end()
-        branch_end(x_ref, positions, gate0, r0.parts[i], own_ref.at[0], cols)
+        branch_end(x_ref, positions, gate0, r0.parts[i], own_ref.at[0], 0, cols)
         swaps.append(
             Swap(own_ref.at[0], middle_ref, cols, swap_out(), frames, swap_sems.at[i], local.at[5, i])
         )
         swaps[i].start()
         if i == 0:
             w1[1].middle()
-    a0 = two(gather_of, middle_ref, by_frames, 0)
+    a0 = parted(gather_of, middle_ref, by_frames, 0)
     for i in range(2):
         swaps[i].wait()
         a0.parts[i].start()
@@ -719,79 +736,83 @@
     w1[1].fifth()
     w1[1].end()
     a0.last()
+    w1[0].near_got(*shards)
+    dy_load.wait()
+    attended_grad(dy_ref, w1_ref, gate1, datt_ref, whole_rows)
     w1[2].last()
     w1[2].fifth()
     w1[2].end()
     for weights in (w0p, w0o, *w1):
         weights.sent()
-    for weights in w1:
+    for weights in w1[1:]:
         weights.near_got(*shards)
-    attended_grad(dy_ref, w1_ref, gate1, datt_ref)
-    a0.fifth()
-    a0.end()
-    a0.sent()
-
-    normalise(middle_ref, gain1, normed1_ref)
-    for group in range(4):
-        project(group, normed1_ref, w1_ref, proj1_ref, group == 0)
+
+    proj1_ref[...] = jnp.zeros_like(proj1_ref)
+    squares = jnp.zeros((T, 1), F32)
+    for piece, cols in zip(a0.parts, halves):
+        piece.fifth()
+        piece.end()
+        squares = project_scaled(middle_ref, w1_ref, gain1, proj1_ref, cols, squares)
+    proj1_ref[...] *= lax.rsqrt(squares / D + EPS)
     attend(proj1_ref, qkg1, att1_ref, True)
     branch(att1_ref, w1_ref, part1_ref, whole_rows)
-    r1 = Reduce(part1_ref, by_frames, OWN, whole_rows, held_ref.at[1], rs_sems.at[2])
+    r1 = Reduce(part1_ref, by_frames, OWN, whole_rows, held_ref.at[1], rs_sems.at[4])
     r1.start()
     grad_cols = ((PC, WC - PC), (0, 384), (384, 384))
     grads1 = [
         WeightGrads(g_ref, cols, far1_ref, g_sems.at[i], near1_ref, gn_sems.at[i]) for i, cols in enumerate(grad_cols)
     ]
-    outw_grads(dy_ref, gate1, att1_ref, g_ref)
-    grads1[0].pair()
     projected_grad(qkg1, proj1_ref, datt_ref, dproj_ref, True)
 
-    r2 = two(reduce_of, by_frames, 2, 3)
+    r2 = parted(reduce_of, by_frames, 2, 5)
     for piece, cols in zip(r2.parts, halves):
         normed_grad(dproj_ref, w1_ref, part_ref, cols)
         piece.start()
+    outw_grads(dy_ref, gate1, att1_ref, g_ref, whole_rows)
+    grads1[0].pair()
+    normalise(middle_ref, gain1, normed1_ref)
+    proj_grads(normed1_ref, dproj_ref, g_ref, grad_cols[1])
+    grads1[1].pair()
     grads1[0].start()
-    for i in (1, 2):
-        proj_grads(normed1_ref, dproj_ref, g_ref, grad_cols[i])
-        grads1[i].pair()
     r2.middle()
+    proj_grads(normed1_ref, dproj_ref, g_ref, grad_cols[2])
+    grads1[2].pair()
     grads1[1].start()
-    r1.middle()
     r2.last()
     grads1[0].middle()
+    a0.sent()
     r2.end()
-    input_grad(middle_ref, frames, dy_ref, frames, gain1, r2.parts[0], sum_ref, own_ref.at[1])
-    a1 = two(gather_of, grad_ref, by_positions, 2)
+    input_grad(middle_ref, frames, dy_ref, frames, gain1, r2.parts[0], sum_ref, own_ref.at[1], 0)
+    a1 = parted(gather_of, grad_ref, by_positions, 4)
     swaps = [
-        Swap(own_ref.at[1], grad_ref, cols, swap_back(), positions, swap_sems.at[2 + i], local.at[5, i])
+        Swap(own_ref.at[1], grad_ref, cols, swap_back(), positions, swap_sems.at[4 + i], local.at[5, i])
         for i, cols in enumerate(halves)
     ]
     for i in range(2):
         swaps[i].start()
+    r1.middle()
+    grads1[0].last()
     r1.last()
-    grads1[0].last()
     for i in range(2):
         swaps[i].wait()
         a1.parts[i].start()
     grads1[1].middle()
     a1.middle()
+    r1.end()
+    branch_end(middle_ref, frames, gate1, r1, mixed_ref, frames, whole_rows)
     grads1[2].start()
     a1.last()
+    a2 = Gather(mixed_ref, by_frames, OWN, whole_rows, ag_sems.at[8])
+    a2.start()
     grads1[1].last()
-    r1.end()
-    branch_end(middle_ref, frames, gate1, r1, own_ref.at[2], whole_rows)
-    keep = pltpu.make_async_copy(own_ref.at[2], mixed_ref.at[rows_at(frames, OWN)], local.at[6, 0])
-    keep.start()
-    keep.wait()
-    a1.fifth()
-    a2 = Gather(mixed_ref, by_frames, OWN, whole_rows, ag_sems.at[4])
-    a2.start()
     grads1[2].middle()
-    a1.end()
-
-    attended_grad(grad_ref, w0_ref, gate0, datt_ref)
+
+    for piece, cols in zip(a1.parts, halves):
+        piece.fifth()
+        piece.end()
+        attended_grad(grad_ref, w0_ref, gate0, datt_ref, cols)
     projected_grad(qkg0, proj0_ref, datt_ref, dproj_ref, False)
-    r3 = two(reduce_of, by_positions, 3, 5)
+    r3 = parted(reduce_of, by_positions, 3, 9)
     for piece, cols in zip(r3.parts, halves):
         normed_grad(dproj_ref, w0_ref, part_ref, cols)
         piece.start()
@@ -805,27 +826,24 @@
     a2.middle()
     proj_grads(normed0_ref, dproj_ref, w0_ref, grad_cols[2])
     grads0[2].pair()
+    grads0[1].start()
     r3.middle()
-    grads0[1].start()
-    outw_grads(grad_ref, gate0, att0_ref, w0_ref)
+    outw_grads(grad_ref, gate0, att0_ref, w0_ref, whole_rows)
     grads0[0].pair()
+    grads0[2].start()
     r3.last()
-    grads0[2].start()
     grads1[2].last()
     grads0[1].middle()
+    grads0[0].start()
     r3.end()
-    input_grad(x_ref, positions, grad_ref, positions, gain0, r3.parts[0], sum_ref, own_ref.at[3])
-    keep = pltpu.make_async_copy(own_ref.at[3], clip_ref.at[rows_at(positions, OWN)], local.at[6, 1])
-    keep.start()
-    grads0[0].start()
-    keep.wait()
-    a3 = two(gather_of, clip_ref, by_positions, 5)
+    input_grad(x_ref, positions, grad_ref, positions, gain0, r3.parts[0], sum_ref, clip_ref, positions)
+    a3 = parted(gather_of, clip_ref, by_positions, 9, False)
     a3.start()
     a2.last()
     grads0[2].middle()
-    grads0[0].middle()
     a3.middle()
     grads0[1].last()
+    grads0[0].middle()
     a3.last()
     grads0[2].last()
     for i in range(3):
@@ -855,13 +873,16 @@
 def local_program(clip_tokens, out_cotangent, proj_weight, out_weight, norm_gain, branch_gate, qk_gain):
     in_vmem = pl.BlockSpec(memory_space=pltpu.VMEM)
     anywhere = pl.BlockSpec(memory_space=pl.ANY)
+    out_shapes = [(T, D), (T, D), (2, SH, PC), (2, SH, WC - PC)]
     tokens = lambda *lead: pltpu.VMEM((*lead, T, D), BF16)
     mixed, clip, gproj, goutw = pl.pallas_call(
         whole,
-        out_shape=[shaped((T, D)), shaped((T, D)), shaped((2, SH, PC)), shaped((2, SH, WC - PC))],
-        in_specs=[in_vmem, in_vmem, anywhere, anywhere, in_vmem, in_vmem, in_vmem],
-        out_specs=[anywhere, anywhere, in_vmem, in_vmem],
+        out_shape=[pltpu.VMEM(shape, BF16) for shape in out_shapes],
+        in_specs=[anywhere] * 4 + [in_vmem] * 3,
+        out_specs=[in_vmem] * 4,
         scratch_shapes=[
+            tokens(),
+            tokens(),
             pltpu.VMEM((D, WC), BF16),
             pltpu.VMEM((D, WC), BF16),
             pltpu.VMEM((D, WC), BF16),
@@ -884,12 +905,12 @@
             pltpu.VMEM((7 * SH, WC), BF16),
             sem(5, 2, 9),
             sem(5, 2, 8),
-            sem(7, 2),
-            sem(7, 2, 9),
-            sem(7, 2, 9),
+            sem(7, 4),
+            sem(13, 2, 9),
+            sem(13, 2, 9),
             sem(6, 2, 9),
             sem(6, 2, 8),
-            sem(4, 2, 2),
+            sem(8, 2, 2),
         ],
         compiler_params=pltpu.CompilerParams(
             vmem_limit_bytes=VMEM_LIMIT, collective_id=0, has_side_effects=True

time: 209 us -> 201 us (0.962)
  Pallas kernels: 201 us -> 196 us
  local copies, waits for them, and re-layouts: 6.09 us -> 3.99 us
    pallas_call x1, Pallas kernels: 201 us -> 196 us  [local_program(): pl.pallas_call(whole, out_shape=[pltpu.VMEM(shape, BF16) for shape in out...]
    unnamed x10 -> x4, local copies, waits for them, and re-layouts: 6.09 us -> 3.99 us
where the time goes in v3:
time: 201 us
  Pallas kernels  196 us (98%)
  local copies, waits for them, and re-layouts  3.99 us (2%)
    pallas_call x1, Pallas kernels, local_program(): pl.pallas_call(whole, out_shape=[pltpu.VMEM(shape, BF16) for shape in out...  196 us

profile of v3, /device:TPU:8, one launch (start us, length us, event | category | flops | bytes accessed | tf_op | source)
XLA Modules:
  0.0 200.5 jit_solution(7745466705159809260)
XLA Ops:
  0.6 195.9 %two_blocks.1 = (bf16[256,3584]{1,0:T(8,128)(2,1)S(1)}, bf16[256,3584]{1,0:T(8,128)(2,1)S(1)}, bf16[2,224,768]{2,1,0:T(8,128)(2,1)S(1)}, bf16[2,224,256]{2,1,0:T(8,128)(2,1)S(1)}) custom-call(bf16[256,3584]{1,0:T(8,128)(2,1)} %bitcast.9, bf16[256,3584]{1,0:T(8,128)(2,1)} %bitcast.10, bf16[2,224,768]{2,1,0:T(8,128)(2,1)} %proj_in.1, ...), custom_call_target="tpu_custom_call" | custom-call | tf_op jit(solution)/shard_map/two_blocks/pallas_call | solution.py:878
  196.5 1.2 copy.15
  197.7 1.2 copy.16
  199.0 0.7 copy.18
  199.7 0.8 copy.17
